TPU v7x, 32 devices: a whole 2x2x4 slice. The times are simulated.
32 devices in a mesh: groups: 2 (over y), cache: 4 (over z), blk: 4 (over x, core).
Axes of the slice: x: 2, y: 2, z: 4, core: 2. Of those that a mesh axis runs over, the one named last changes fastest.
Arguments:
- queries: bfloat16 [8, 512, 2048], P(('groups', 'cache'), 'blk'), parts along dimension 0, may hold values from -6 to 6
- kv_new: bfloat16 [8, 512, 1024], P(('groups', 'cache'), 'blk'), parts along dimension 0, may hold values from -6 to 6
- page_pool: bfloat16 [8, 128, 8, 1024], P(('groups', 'cache')), parts along dimension 0, may hold values from -6 to 6
- page_owner: int32 [8, 4, 32, 1], P(('groups', 'cache'), 'blk'), parts along dimension 0, may hold values from 0 to 3; in each aligned block of 32 rows (0 to 31, 32 to 63, ..., all dimensions but the last counted through in order) at most 16 rows name the same one
- page_slot: int32 [8, 4, 32], P(('groups', 'cache'), 'blk'), parts along dimension 0, may hold values from 0 to 127
- prefix_len: int32 [8], P(('groups', 'cache')), parts along dimension 0, may hold values from 1 to 1024, 2048 in all
- suffix_len: int32 [8], P(('groups', 'cache')), parts along dimension 0, may hold values from 1 to 512, 1536 in all
- ssm_in: bfloat16 [8, 512, 2048], P(('groups', 'cache'), 'blk'), parts along dimension 0, may hold values from -6 to 6
- b_in: bfloat16 [8, 512, 128], P(('groups', 'cache'), 'blk'), parts along dimension 0, may hold values from -4 to 4
- c_in: bfloat16 [8, 512, 128], P(('groups', 'cache'), 'blk'), parts along dimension 0, may hold values from -4 to 4
- step_size: float32 [8, 512, 32], P(('groups', 'cache'), 'blk'), parts along dimension 0, may hold values from 0.01 to 0.1
- decay_rate: float32 [32], replicated, may hold values from 0.001953125 to 4
- skip_gain: float32 [32], replicated, may hold values from 0.5 to 1.5
- prior_state: float32 [8, 32, 64, 128], P(('groups', 'cache')), parts along dimension 0, may hold values from -4 to 4
Outputs:
- attn_out: bfloat16 [8, 512, 2048], P(('groups', 'cache'), 'blk'), parts along dimension 0
- ssm_out: bfloat16 [8, 512, 2048], P(('groups', 'cache'), 'blk'), parts along dimension 0
There are 2 independent parts, one for each index of `groups`. A program takes and returns all parts, laid end to end along the dimension named above; an argument that names none is the same for every part. Nothing has to cross between parts.
Inputs may be any that keep to these rules, and one draw needn't show every extreme that they name: `page_owner`: among the 32 pages of one request at one index of blk, no owner is named more than 16 times, a bound that some block reaches. `prefix_len`: the largest is 1024. `suffix_len`: the largest is 512.
All inputs are finite; a program needn't handle non-finite values. No bound on the sum of `prefix_len` or of `suffix_len` on one device may be relied on, other than what follows from the above.
Results may differ from a plain program's by a relative error of at most 0.008.
Values may be sent and summed in bfloat16 or wider, within the bound.
A program may use at most 128 MiB of HBM per device.

v0:
```python
import functools
import math

import jax
import jax.numpy as jnp
from jax import lax
from jax.experimental import pallas as pl
from jax.experimental.pallas import tpu as pltpu
from jax.sharding import PartitionSpec as P

QH = 16
KVH = 4
HD = 128
SH = 32
HP = 64
NS = 128
PAGE = 8
GROUP = QH // KVH
NEG = -1e30
F32 = jnp.float32
BF16 = jnp.bfloat16


def remote(src, dst, send_sem, recv_sem, device):
    return pltpu.make_async_remote_copy(
        src_ref=src,
        dst_ref=dst,
        send_sem=send_sem,
        recv_sem=recv_sem,
        device_id=device,
        device_id_type=pl.DeviceIdType.MESH,
    )


def nt(a, b, **kw):
    return lax.dot_general(a, b, (((1,), (1,)), ((), ())), preferred_element_type=F32, **kw)


def nn(a, b, **kw):
    return jnp.dot(a, b, preferred_element_type=F32, **kw)


def iota(shape, axis):
    return lax.broadcasted_iota(jnp.int32, shape, axis)


def kernel(
    n, nb, cap, lists,
    plen, slen, codes, q, kv, pool, x, b_t, b_rows, c_rows, dt, rate, skip, prior,
    attn_o, ssm_o,
    tiles, combs, sendbuf, recv, qbuf, kbuf, vbuf, mbuf, lbuf, accbuf, obuf,
    lx, dx, l_t, dt_t, sbuf, ybuf, hin, hout,
    ts, tr, cs, cr, ps, pr, qs, qr, ks, kr, vs, vr, os, orr, hs, hr,
):
    me = lax.axis_index("cache")
    j = lax.axis_index("blk")
    tok = x.shape[0]
    width = GROUP * HD
    prefix_limit = plen[0]
    suffix_limit = slen[0]

    def zpeer(d):
        return lax.rem(me + d, n)

    def bpeer(e):
        return lax.rem(j + e, nb)

    barrier = pltpu.get_barrier_semaphore()

    def greet_z(d, carry):
        pl.semaphore_signal(barrier, inc=1, device_id={"cache": zpeer(d)}, device_id_type=pl.DeviceIdType.MESH)
        return carry

    def greet_b(e, carry):
        pl.semaphore_signal(barrier, inc=1, device_id={"blk": bpeer(e)}, device_id_type=pl.DeviceIdType.MESH)
        return carry

    lax.fori_loop(1, n, greet_z, 0)
    lax.fori_loop(1, nb, greet_b, 0)
    pl.semaphore_wait(barrier, n - 1 + nb - 1)

    def tile_copy(e):
        return remote(codes, tiles.at[j], ts.at[e], tr.at[e], {"blk": bpeer(e)})

    def q_copy(e):
        to = bpeer(e)
        return remote(q.at[:, pl.ds(pl.multiple_of(to * width, width), width)], qbuf.at[j], qs.at[e], qr.at[e], {"blk": to})

    def k_copy(e):
        to = bpeer(e)
        return remote(kv.at[:, pl.ds(pl.multiple_of(to * HD, HD), HD)], kbuf.at[j], ks.at[e], kr.at[e], {"blk": to})

    def v_copy(e):
        to = bpeer(e)
        return remote(kv.at[:, pl.ds(pl.multiple_of(KVH * HD + to * HD, HD), HD)], vbuf.at[j], vs.at[e], vr.at[e], {"blk": to})

    def comb_copy(d):
        return remote(combs.at[0], combs.at[d], cs.at[d], cr.at[d], {"cache": zpeer(d)})

    def page_copy(d):
        return remote(sendbuf.at[d], recv.at[d], ps.at[d], pr.at[d], {"cache": zpeer(d)})

    def state_copy():
        return remote(hout, hin, hs, hr, {"blk": bpeer(1)})

    def out_copy(e):
        to = bpeer(e)
        return remote(obuf.at[to], attn_o.at[:, pl.ds(pl.multiple_of(j * width, width), width)], os.at[e], orr.at[e], {"blk": to})

    def each_b(what):
        def body(e, carry):
            what(e)
            return carry
        lax.fori_loop(1, nb, body, 0)

    def each_z(what, low=1, high=n):
        def body(d, carry):
            what(d)
            return carry
        lax.fori_loop(low, high, body, 0)

    each_b(lambda e: tile_copy(e).start())
    each_b(lambda e: (q_copy(e).start(), k_copy(e).start(), v_copy(e).start()))
    tiles[j] = codes[...]
    each_b(lambda e: tile_copy(e).wait_recv())
    combs[0] = jnp.sum(tiles[...], axis=0)
    each_z(lambda d: comb_copy(d).start())
    qbuf[j] = q[:, pl.ds(pl.multiple_of(j * width, width), width)]
    kbuf[j] = kv[:, pl.ds(pl.multiple_of(j * HD, HD), HD)]
    vbuf[j] = kv[:, pl.ds(pl.multiple_of(KVH * HD + j * HD, HD), HD)]

    lanes = combs.shape[2]
    before = jnp.where(iota((lanes, lanes), 0) < iota((lanes, lanes), 1), 1.0, 0.0).astype(BF16)

    def placing(slot, owner):
        named = combs[slot, 0:1, :] == owner + 1
        flags = jnp.broadcast_to(jnp.where(named, 1.0, 0.0), (16, lanes)).astype(BF16)
        rank = nn(flags, before)[0:1].astype(jnp.int32)
        return jnp.where((rank == iota((cap, lanes), 0)) & named, 1.0, 0.0).astype(BF16)

    def packed(slot):
        spots = pool.shape[0]
        wants = jnp.where(combs[slot, 1:2, :] == iota((spots, lanes), 0), 1.0, 0.0).astype(BF16)
        chosen = nt(placing(slot, me), wants).astype(BF16)
        return nn(chosen, pool[...]).astype(BF16)

    def answer(d):
        comb_copy(d).wait_recv()
        back = n - d
        sendbuf[back] = packed(d)
        page_copy(back).start()

    each_z(answer)
    recv[0] = packed(0)

    tri = jnp.where(iota((tok, tok), 0) >= iota((tok, tok), 1), 1.0, 0.0)
    exact = dict(precision=lax.Precision.HIGHEST)
    spread = jnp.where(iota((SH, SH * HP), 0) == iota((SH, SH * HP), 1) // HP, 1.0, 0.0)
    logs = nn(tri, dt[...] * (-rate[...]), **exact)
    lx[...] = nn(logs, spread, **exact)
    dx[...] = nn(dt[...], spread, **exact)
    l_t[...] = logs.T
    dt_t[...] = dt[...].T
    gram = nt(c_rows[...], b_rows[...])
    lower = iota((tok, tok), 0) >= iota((tok, tok), 1)
    first_half = iota((tok, 2 * HP), 1) < HP

    def pair_local(pair, carry):
        at = pl.ds(pl.multiple_of(pair * 2 * HP, 2 * HP), 2 * HP)
        xs = x[:, at]
        xf = xs.astype(F32)
        ltile = lx[:, at]

        def mixed(which):
            column = ltile[:, which * HP : which * HP + 1]
            row = l_t[pl.ds(2 * pair + which, 1), :]
            step = dt_t[pl.ds(2 * pair + which, 1), :]
            decay = jnp.exp(jnp.where(lower, column - row, NEG))
            return nn((gram * decay * step).astype(BF16), xs)

        ybuf[:, at] = jnp.where(first_half, mixed(0), mixed(1)) + skip[:, at] * xf
        scaled = (jnp.exp(ltile[tok - 1 : tok] - ltile) * dx[:, at] * xf).astype(BF16)
        sbuf[:, at] = nn(b_t[...], scaled)
        return carry

    lax.fori_loop(0, SH // 2, pair_local, 0)

    def chain():
        @pl.when(j == 0)
        def _():
            def fill(pair, carry):
                at = pl.ds(pl.multiple_of(pair * 2 * HP, 2 * HP), 2 * HP)
                hin[:, at] = prior[at, :].T.astype(BF16)
                return carry
            lax.fori_loop(0, SH // 2, fill, 0)

        @pl.when(j > 0)
        def _():
            state_copy().wait_recv()

        def onward(pair, carry):
            at = pl.ds(pl.multiple_of(pair * 2 * HP, 2 * HP), 2 * HP)
            decay = jnp.exp(lx[tok - 1 : tok, at])
            hout[:, at] = (decay * hin[:, at].astype(F32) + sbuf[:, at]).astype(BF16)
            return carry

        @pl.when(j < nb - 1)
        def _():
            lax.fori_loop(0, SH // 2, onward, 0)
            state_copy().start()

        alive = j * tok + iota((tok, 2 * HP), 0) < suffix_limit

        def read(pair, carry):
            at = pl.ds(pl.multiple_of(pair * 2 * HP, 2 * HP), 2 * HP)
            total = ybuf[:, at] + jnp.exp(lx[:, at]) * nn(c_rows[...], hin[:, at])
            ssm_o[:, at] = jnp.where(alive, total, 0.0).astype(BF16)
            return carry

        lax.fori_loop(0, SH // 2, read, 0)

    scale = 1.0 / math.sqrt(HD)
    rows = GROUP * tok

    def attend(b, keys, values, seen, first=False, last=False):
        qb = jnp.concatenate([qbuf[b, :, h * HD : (h + 1) * HD] for h in range(GROUP)], axis=0)
        scores = jnp.where(seen, nt(qb, keys) * scale, NEG)
        top = jnp.max(scores, axis=1, keepdims=True)
        if not first:
            old = mbuf[b]
            top = jnp.maximum(top, old)
            factor = jnp.exp(old - top)
        weights = jnp.exp(scores - top)
        total = jnp.sum(weights, axis=1, keepdims=True)
        mixed = nn(weights.astype(BF16), values)
        if not first:
            total = total + lbuf[b] * factor
            mixed = mixed + accbuf[b] * factor
        if not last:
            mbuf[b] = top
            lbuf[b] = total
            accbuf[b] = mixed
            return None
        alive = b * tok + lax.rem(iota((rows, HD), 0), tok) < suffix_limit
        return jnp.where(alive, mixed / total, 0.0).astype(BF16)

    each_b(lambda e: (q_copy(e).wait_recv(), k_copy(e).wait_recv(), v_copy(e).wait_recv()))

    def suffix_phase():
        keys = kbuf[...].reshape(nb * tok, HD)
        values = vbuf[...].reshape(nb * tok, HD)

        def block(b, carry):
            where_q = b * tok + lax.rem(iota((rows, nb * tok), 0), tok)
            where_k = iota((rows, nb * tok), 1)
            attend(b, keys, values, (where_k <= where_q) & (where_k < suffix_limit), first=True)
            return carry

        lax.fori_loop(0, nb, block, 0)

    per = max(1, n // 4)
    groups = n // per
    order = [0, 1, 3, 2] if groups == 4 else list(range(groups))

    def page_phase(g, last):
        if g == 0:
            each_z(lambda d: page_copy(d).wait_recv(), 1, per)
        else:
            each_z(lambda d: page_copy(d).wait_recv(), g * per, (g + 1) * per)
        span = per * cap
        slots = [lax.rem(me - d + n, n) for d in range(g * per, (g + 1) * per)]
        place = jnp.concatenate([placing(0, o) for o in slots], axis=0)
        k = iota((16, lanes), 1)
        number = lax.rem(k, lists) * nb + k // lists + 1
        page = nt(number.astype(F32).astype(BF16), jnp.concatenate([place] * PAGE, axis=0))[0:1].astype(jnp.int32)
        offset = iota((1, PAGE * span), 1) // span
        seen = (page > 0) & ((page - 1) * PAGE + offset < prefix_limit)

        def part(low):
            return jnp.concatenate(
                [
                    recv[g * per : (g + 1) * per, :, low + i * HD : low + (i + 1) * HD].reshape(span, HD)
                    for i in range(PAGE)
                ],
                axis=0,
            )

        keys = part(0)
        values = part(PAGE * HD)

        def block(e, carry):
            b = bpeer(e)
            out = attend(b, keys, values, seen, last=last)
            if last:
                for h in range(GROUP):
                    obuf[b, :, h * HD : (h + 1) * HD] = out[h * tok : (h + 1) * tok]

                @pl.when(e < nb)
                def _():
                    out_copy(e).start()
            return carry

        lax.fori_loop(1, nb + 1, block, 0)

    for phase in range(groups + 1):
        if phase < nb:
            pl.when(j == phase)(chain)
        if phase == 0:
            suffix_phase()
        else:
            page_phase(order[phase - 1], phase == groups)
    attn_o[:, pl.ds(pl.multiple_of(j * width, width), width)] = obuf[j]

    each_b(lambda e: out_copy(e).wait())
    each_b(lambda e: (tile_copy(e).wait_send(), q_copy(e).wait_send(), k_copy(e).wait_send(), v_copy(e).wait_send()))
    each_z(lambda d: (comb_copy(d).wait_send(), page_copy(d).wait_send()))

    @pl.when(j < nb - 1)
    def _():
        state_copy().wait_send()


def local(
    queries, kv_new, page_pool, page_owner, page_slot, prefix_len, suffix_len,
    ssm_in, b_in, c_in, step_size, decay_rate, skip_gain, prior_state,
):
    n = lax.axis_size("cache")
    nb = lax.axis_size("blk")
    j = lax.axis_index("blk")
    tok = queries.shape[1]
    lists = page_owner.shape[2]
    lanes = nb * lists
    cap = max(16, max(2, 2 * lists // n) * nb)
    half = KVH * HD
    pages = page_pool[0]
    spots = pages.shape[0]
    chosen = jnp.stack(
        [
            lax.dynamic_slice_in_dim(pages, j * HD, HD, 2),
            lax.dynamic_slice_in_dim(pages, half + j * HD, HD, 2),
        ],
        axis=1,
    ).reshape(spots, 2 * PAGE * HD)
    if spots < 128:
        chosen = jnp.pad(chosen, ((0, 128 - spots), (0, 0)))
    pair = jnp.stack([page_owner[0, 0, :, 0] + 1, page_slot[0, 0]])
    mine = jnp.arange(lanes, dtype=jnp.int32) // lists == j
    codes = jnp.where(mine[None], jnp.tile(pair, (1, nb)), 0)
    codes = jnp.pad(codes, ((0, 6), (0, 0)))
    vmem = pl.BlockSpec(memory_space=pltpu.VMEM)
    smem = pl.BlockSpec(memory_space=pltpu.SMEM)
    dma = pltpu.SemaphoreType.DMA
    wide = SH * HP
    rows = GROUP * tok
    attn, ssm = pl.pallas_call(
        functools.partial(kernel, n, nb, cap, lists),
        out_shape=(
            jax.ShapeDtypeStruct((tok, QH * HD), BF16),
            jax.ShapeDtypeStruct((tok, wide), BF16),
        ),
        in_specs=[smem, smem] + [vmem] * 12,
        out_specs=(vmem, vmem),
        scratch_shapes=[
            pltpu.VMEM((nb, 8, lanes), jnp.int32),
            pltpu.VMEM((n, 8, lanes), jnp.int32),
            pltpu.VMEM((n, cap, 2 * PAGE * HD), BF16),
            pltpu.VMEM((n, cap, 2 * PAGE * HD), BF16),
            pltpu.VMEM((nb, tok, GROUP * HD), BF16),
            pltpu.VMEM((nb, tok, HD), BF16),
            pltpu.VMEM((nb, tok, HD), BF16),
            pltpu.VMEM((nb, rows, 1), F32),
            pltpu.VMEM((nb, rows, 1), F32),
            pltpu.VMEM((nb, rows, HD), F32),
            pltpu.VMEM((nb, tok, GROUP * HD), BF16),
            pltpu.VMEM((tok, wide), F32),
            pltpu.VMEM((tok, wide), F32),
            pltpu.VMEM((SH, tok), F32),
            pltpu.VMEM((SH, tok), F32),
            pltpu.VMEM((NS, wide), F32),
            pltpu.VMEM((tok, wide), F32),
            pltpu.VMEM((NS, wide), BF16),
            pltpu.VMEM((NS, wide), BF16),
            dma((nb,)), dma((nb,)), dma((n,)), dma((n,)), dma((n,)), dma((n,)),
            dma((nb,)), dma((nb,)), dma((nb,)), dma((nb,)), dma((nb,)), dma((nb,)),
            dma((nb,)), dma((nb,)), dma, dma,
        ],
        compiler_params=pltpu.CompilerParams(
            collective_id=0, has_side_effects=True, vmem_limit_bytes=56 * 1024 * 1024
        ),
    )(
        prefix_len, suffix_len, codes, queries[0], kv_new[0], chosen, ssm_in[0],
        b_in[0].T, b_in[0], c_in[0], step_size[0], decay_rate[None, :],
        jnp.repeat(skip_gain, HP)[None, :], prior_state[0].reshape(wide, NS),
    )
    return attn[None], ssm[None]


def solution(mesh):
    in_specs = (
        P(("groups", "cache"), "blk", None),
        P(("groups", "cache"), "blk", None),
        P(("groups", "cache"), None, None, None),
        P(("groups", "cache"), "blk", None, None),
        P(("groups", "cache"), "blk", None),
        P(("groups", "cache")),
        P(("groups", "cache")),
        P(("groups", "cache"), "blk", None),
        P(("groups", "cache"), "blk", None),
        P(("groups", "cache"), "blk", None),
        P(("groups", "cache"), "blk", None),
        P(),
        P(),
        P(("groups", "cache"), None, None, None),
    )
    out_specs = (P(("groups", "cache"), "blk", None), P(("groups", "cache"), "blk", None))
    return jax.shard_map(local, mesh=mesh, in_specs=in_specs, out_specs=out_specs, check_vma=False)
```

profile of v0, /device:TPU:21, one launch (start us, length us, event | category | flops | bytes accessed | tf_op | source)
XLA Modules:
  0.0 76.4 jit_solution(11796666695405188262)
XLA Ops:
  1.9 0.7 add_bitcast_fusion
  2.6 0.7 pad_add_fusion
  3.3 0.1 tile.10
  3.4 0.6 pad.4.codes
  4.0 0.7 broadcast_in_dim.28
  4.7 0.7 broadcast_in_dim_reshape.3.skip
  5.4 1.5 %copy.17.b_t = bf16[128,128]{1,0:T(8,128)(2,1)} copy(bf16[128,128]{0,1:T(8,128)(2,1)} %bitcast.33) | data formatting | bytes 65536 | tf_op jit(solution)/shard_map/transpose | solution.py:392
  6.8 1.4 %copy.16 = f32[1,128,32]{2,1,0:T(8,128)} copy(f32[1,128,32]{1,2,0:T(8,128)} %param.24) | data formatting | bytes 32768 | tf_op args[10]
  8.3 1.1 %dynamic-slice_bitcast_fusion.1 = (bf16[128,1,8,128]{3,2,1,0:T(8,128)(2,1)S(1)}, bf16[128,1,8,128]{3,2,1,0:T(8,128)(2,1)S(1)}) fusion(bf16[1,128,8,1024]{3,2,1,0:T(8,128)(2,1)} %param.16, s32[]{:T(128)S(6)} %select_n.21, s32[]{:T(128)S(6)} %select_n.22), kind=kLoop, calls=%fused_computation.3 | loop fusion | bytes 1048584 | tf_op jit(solution)/shard_map/stack | solution.py:337
  9.4 0.1 pad_maximum_fusion
  9.5 0.9 %copy.20 = bf16[16,8,16,128]{3,1,2,0:T(8,128)(2,1)} copy(bf16[16,8,16,128]{3,2,1,0:T(8,128)(2,1)S(1)} %bitcast.24) | data formatting | bytes 1048576
  10.4 62.2 %shard_map.149 = (bf16[128,2048]{1,0:T(8,128)(2,1)}, bf16[128,2048]{1,0:T(8,128)(2,1)}) custom-call(s32[1]{0:T(128)S(6)} %copy.23.plen, s32[1]{0:T(128)S(6)} %copy.24.slen, s32[8,128]{1,0:T(8,128)} %pad.4.codes, bf16[128,2048]{1,0:T(8,128)(2,1)} %bitcast.29, bf16[128,1024]{1,0:T(8,128)(2,1)} %bitcast.31, bf16[128,2048]{1,0:T(8,128)(2,1)} %bitcast.25, ...), custom_call_target="tpu_custom_call" | custom-call | tf_op jit(solution)/shard_map/pallas_call | solution.py:355
  72.6 1.9 %copy.25 = bf16[1,128,2048]{2,1,0:T(8,128)(2,1)} copy(bf16[1,128,2048]{2,1,0:T(8,128)(2,1)} %bitcast.28) | data formatting | bytes 1048576
  74.5 1.9 %copy.26 = bf16[1,128,2048]{2,1,0:T(8,128)(2,1)} copy(bf16[1,128,2048]{2,1,0:T(8,128)(2,1)} %bitcast.27) | data formatting | bytes 1048576
  (3 shorter events, 0.0 us)
where the time goes:
time: 76.8 us; the launch traced here: 76.4 us
  Pallas kernels  62.2 us (81%)
  local copies, waits for them, and re-layouts  10.8 us (14%)
  between operations  1.96 us (3%)
  other arithmetic  1.43 us (2%)
    pallas_call x1, Pallas kernels, local(): pl.pallas_call(functools.partial(kernel, n, nb, cap, lists), out_shape=(j...  62.2 us
    unnamed x4, local copies, waits for them, and re-layouts  6.14 us

commit v1 on v0

v1 whole, which is shorter than its diff:
```python
import functools
import math

import jax
import jax.numpy as jnp
from jax import lax
from jax.experimental import pallas as pl
from jax.experimental.pallas import tpu as pltpu
from jax.sharding import PartitionSpec as P

QH = 16
KVH = 4
HD = 128
SH = 32
HP = 64
NS = 128
PAGE = 8
GROUP = QH // KVH
NEG = -1e30
CHUNK = 16
F32 = jnp.float32
BF16 = jnp.bfloat16


def remote(src, dst, send_sem, recv_sem, device):
    return pltpu.make_async_remote_copy(
        src_ref=src,
        dst_ref=dst,
        send_sem=send_sem,
        recv_sem=recv_sem,
        device_id=device,
        device_id_type=pl.DeviceIdType.MESH,
    )


def nt(a, b):
    return lax.dot_general(a, b, (((1,), (1,)), ((), ())), preferred_element_type=F32)


def nn(a, b):
    return jnp.dot(a, b, preferred_element_type=F32)


def iota(shape, axis):
    return lax.broadcasted_iota(jnp.int32, shape, axis)


def thirds(v):
    hi = v.astype(BF16).astype(F32)
    rest = v - hi
    mid = rest.astype(BF16).astype(F32)
    return [hi, mid, (rest - mid).astype(BF16).astype(F32)]


def phases_of(total, cap):
    found, done = [], 0
    for have in [cap - CHUNK, cap]:
        if have <= 0:
            continue
        late = total // cap * (cap - have) + max(total % cap - have, 0)
        ready = (total - late) // 16 * 16
        if ready > done:
            found.append((done, ready, have))
            done = ready
    return found


def kernel(
    n, nb, cap, lists, spots,
    plen, slen, owner, slot, q, kv, pool, x_hbm, b_rows, c_rows, dt_t, rate, skip, prior_hbm,
    attn_o, ssm_o,
    code, codes, praw, pf_k, pf_v, pmat, sendbuf, recv, qbuf, kbuf, vbuf, kx, vstage, vt, mbuf, lbuf, accbuf, obuf,
    x, prior, afull, skipf, xp, sbuf, ybuf, hin, hout,
    loc, cs, cr, ps, pr, qs, qr, ks, kr, vs, vr, os, orr, hs, hr,
):
    me = lax.axis_index("cache")
    j = lax.axis_index("blk")
    tok = x.shape[0]
    wide = x.shape[1]
    width = GROUP * HD
    half = KVH * HD
    lanes = code.shape[1]
    rows = GROUP * tok
    prefix_limit = plen[0]
    suffix_limit = slen[0]
    chunks = cap // CHUNK

    def zpeer(d):
        return lax.rem(me + d, n)

    def bpeer(e):
        return lax.rem(j + e, nb)

    def cols(at, size):
        return pl.ds(pl.multiple_of(at, 128), size)

    loads = [
        pltpu.make_async_copy(x_hbm, x, loc.at[0]),
        pltpu.make_async_copy(pool.at[:, cols(j * HD, HD)], praw.at[0], loc.at[1]),
        pltpu.make_async_copy(pool.at[:, cols(half + j * HD, HD)], praw.at[1], loc.at[2]),
        pltpu.make_async_copy(q.at[:, cols(j * width, width)], qbuf.at[j], loc.at[3]),
        pltpu.make_async_copy(kv.at[:, cols(j * HD, HD)], kbuf.at[j], loc.at[4]),
        pltpu.make_async_copy(kv.at[:, cols(half + j * HD, HD)], vbuf.at[j], loc.at[5]),
    ]
    prior_load = pltpu.make_async_copy(prior_hbm, prior, loc.at[6])
    barrier = pltpu.get_barrier_semaphore()

    def greet(k, carry):
        peer = {"cache": zpeer(k // nb), "blk": bpeer(lax.rem(k, nb))}
        pl.semaphore_signal(barrier, inc=1, device_id=peer, device_id_type=pl.DeviceIdType.MESH)
        return carry

    lax.fori_loop(1, n * nb, greet, 0)
    for load in loads:
        load.start()

    @pl.when(j == 0)
    def _():
        prior_load.start()

    mine = iota((1, lanes), 1) // lists == j
    code[...] = jnp.zeros_like(code)
    code[0:1, :] = jnp.where(mine, jnp.concatenate([owner[...]] * nb, axis=1) + 1, 0)
    code[1:2, :] = jnp.where(mine, jnp.concatenate([slot[...]] * nb, axis=1), 0)
    codes[me, j] = code[...]

    dt = dt_t[...].T
    fall = jnp.concatenate(thirds(dt * (-rate[...])), axis=0).astype(BF16)
    tri = jnp.where(iota((tok, 3 * tok), 0) >= lax.rem(iota((tok, 3 * tok), 1), tok), 1.0, 0.0).astype(BF16)
    logs = nn(tri, fall)
    gains = jnp.concatenate([jnp.exp(logs), jnp.broadcast_to(skip[...], (16, SH))], axis=0)
    a3 = jnp.concatenate(thirds(gains), axis=1).astype(BF16)
    b3 = jnp.concatenate(thirds(jnp.exp(-logs) * dt), axis=1).astype(BF16)
    lower = iota((tok, tok), 0) >= iota((tok, tok), 1)
    gram = jnp.where(lower, nt(c_rows[...], b_rows[...]), 0.0).astype(BF16)
    readout = jnp.concatenate([gram, c_rows[...]], axis=1)
    b_t = b_rows[...].astype(F32).T.astype(BF16)
    part = 2 * HD
    parts = wide // part

    loads[0].wait()

    def own_block(i, carry):
        at = cols(i * part, part)
        heads = lax.rem(iota((3 * SH, part), 0), SH)
        spread = jnp.where(heads == iota((3 * SH, part), 1) // HP + i * (part // HP), 1.0, 0.0).astype(BF16)
        grown = nn(a3, spread)
        afull[:, at] = grown[0:tok]
        skipf[:, at] = grown[tok : tok + 8]
        scaled = (nn(b3, spread) * x[:, at].astype(F32)).astype(BF16)
        xp[:, at] = scaled
        sbuf[:, at] = nn(b_t, scaled)
        return carry

    lax.fori_loop(0, parts, own_block, 0)

    def onward(i, carry):
        at = cols(i * part, part)
        hout[:, at] = (afull[tok - 1 : tok, at] * (hin[:, at].astype(F32) + sbuf[:, at])).astype(BF16)
        return carry

    @pl.when(j == 0)
    def _():
        prior_load.wait()

        def fill(i, carry):
            at = cols(i * HD, HD)
            hin[:, at] = prior[at, :].T.astype(BF16)
            return carry

        lax.fori_loop(0, wide // HD, fill, 0)
        lax.fori_loop(0, parts, onward, 0)

    loads[1].wait()
    loads[2].wait()
    pf_k[...] = praw[0].astype(F32)
    pf_v[...] = praw[1].astype(F32)
    if spots < pmat.shape[0]:
        pmat[...] = jnp.zeros_like(pmat)
    for i in range(PAGE):
        at = pl.ds(i, spots, stride=PAGE)
        pmat[0:spots, i * HD : (i + 1) * HD] = pf_k[at, :].astype(BF16)
        pmat[0:spots, (PAGE + i) * HD : (PAGE + i + 1) * HD] = pf_v[at, :].astype(BF16)

    pl.semaphore_wait(barrier, n * nb - 1)

    def code_copy(k):
        peer = {"cache": zpeer(k // nb), "blk": bpeer(lax.rem(k, nb))}
        return remote(code, codes.at[me, j], cs.at[k], cr.at[k], peer)

    def q_copy(e):
        to = bpeer(e)
        return remote(q.at[:, cols(to * width, width)], qbuf.at[j], qs.at[e], qr.at[e], {"blk": to})

    def k_copy(e):
        to = bpeer(e)
        return remote(kv.at[:, cols(to * HD, HD)], kbuf.at[j], ks.at[e], kr.at[e], {"blk": to})

    def v_copy(e):
        to = bpeer(e)
        return remote(kv.at[:, cols(half + to * HD, HD)], vbuf.at[j], vs.at[e], vr.at[e], {"blk": to})

    def page_copy(d, c):
        at = pl.ds(c * CHUNK, CHUNK)
        return remote(sendbuf.at[d, at], recv.at[d, at], ps.at[d, c], pr.at[d, c], {"cache": zpeer(d)})

    def state_copy():
        return remote(hout, hin, hs, hr, {"blk": bpeer(1)})

    def out_copy(e):
        to = bpeer(e)
        return remote(obuf.at[to], attn_o.at[:, cols(j * width, width)], os.at[e], orr.at[e], {"blk": to})

    def each(what, low, high):
        if high - low <= 4:
            for i in range(low, high):
                what(i)
            return

        def body(i, carry):
            what(i)
            return carry

        lax.fori_loop(low, high, body, 0)

    def each_code(what):
        def body(k, carry):
            what(k)
            return carry

        lax.fori_loop(1, n * nb, body, 0)

    each_code(lambda k: code_copy(k).start())

    @pl.when(j == 0)
    def _():
        state_copy().start()

    each(lambda e: (k_copy(e).start(), v_copy(e).start(), q_copy(e).start()), 1, nb)

    before = jnp.where(iota((lanes, lanes), 0) < iota((lanes, lanes), 1), 1.0, 0.0).astype(BF16)

    def comb(r):
        return jnp.sum(codes[r], axis=0)

    def ranked(named):
        flags = jnp.broadcast_to(jnp.where(named, 1.0, 0.0), (16, lanes)).astype(BF16)
        return nn(flags, before)[0:1].astype(jnp.int32)

    def onehot(flag):
        return jnp.where(flag, 1.0, 0.0).astype(BF16)

    each_code(lambda k: code_copy(k).wait_recv())
    spread_spots = pmat.shape[0]

    def answer(d):
        pair = comb(zpeer(d))
        named = pair[0:1] == me + 1
        place = onehot((ranked(named) == iota((cap, lanes), 0)) & named)
        wants = onehot(pair[1:2] == iota((spread_spots, lanes), 0))
        chosen = nt(place, wants).astype(BF16)
        for i in range(2 * PAGE * HD // part):
            sendbuf[d, :, i * part : (i + 1) * part] = nn(chosen, pmat[:, i * part : (i + 1) * part]).astype(BF16)
        page_copy(d, 0).start()

    each(answer, 1, n)
    for c in range(1, chunks):
        each(lambda d: page_copy(d, c).start(), 1, n)

    pair = comb(me)
    back = me + 1 - pair[0:1]
    away = jnp.where(back < 0, back + n, back)
    rank = jnp.zeros((1, lanes), jnp.int32)

    def add_rank(d, rank):
        named = away == d
        return rank + jnp.where(named, ranked(named), 0)

    if n <= 8:
        for d in range(1, n):
            rank = add_rank(d, rank)
    else:
        rank = lax.fori_loop(1, n, add_rank, rank)
    lane = iota((1, lanes), 1)
    turn = jnp.where(away == 0, 0, rank // CHUNK) * lanes + lane
    turn_f = turn.astype(F32)
    turn_col = jnp.broadcast_to(turn_f, (lanes, lanes)).T
    ahead = jnp.where(turn_col < turn_f, 1.0, 0.0)
    spot = jnp.sum(ahead, axis=0, keepdims=True).astype(jnp.int32)
    sorted_f = jnp.where(iota((lanes, lanes), 0) == spot, 1.0, 0.0)
    sorting = sorted_f.astype(BF16)
    number = (lax.rem(lane, lists) * nb + lane // lists).astype(F32)
    first_row = jnp.sum(sorted_f * number, axis=1, keepdims=True).astype(jnp.int32) * PAGE
    own_wants = onehot((pair[1:2] == iota((spread_spots, lanes), 0)) & (away == 0))
    places = [onehot((rank == iota((cap, lanes), 0)) & (away == d)) for d in range(1, n)]

    def read_block():
        alive = j * tok + iota((tok, part), 0) < suffix_limit

        def body(i, carry):
            at = cols(i * part, part)
            both = jnp.concatenate([xp[:, at], hin[:, at]], axis=0)
            total = afull[:, at] * nn(readout, both) + skipf[0:1, at] * x[:, at].astype(F32)
            ybuf[:, at] = jnp.where(alive, total, 0.0).astype(BF16)
            return carry

        lax.fori_loop(0, parts, body, 0)

    def chain():
        state_copy().wait_recv()

        @pl.when(j < nb - 1)
        def _():
            lax.fori_loop(0, parts, onward, 0)
            state_copy().start()

        read_block()

    pl.when(j == 0)(read_block)
    pl.when(j == 1)(chain)

    rate2 = math.log2(math.e) / math.sqrt(HD)
    first_lane = iota((1, HD), 1) == 0
    one_column = jnp.broadcast_to(jnp.where(first_lane, 1.0, 0.0), (tok, HD)).astype(BF16)

    def queries(b):
        pieces = [jnp.concatenate([qbuf[b, :, h * HD : (h + 1) * HD], one_column], axis=1) for h in range(GROUP)]
        return jnp.concatenate(pieces, axis=0)

    def bias(visible, size):
        column = jnp.where(visible, 0.0, NEG)
        return jnp.where(first_lane, jnp.broadcast_to(column, (size, HD)), 0.0).astype(BF16)

    for load in loads[3:]:
        load.wait()
    each(lambda e: (k_copy(e).wait_recv(), v_copy(e).wait_recv(), q_copy(e).wait_recv()), 1, nb)

    for b in range(nb):
        kx[b * tok : (b + 1) * tok, 0:HD] = kbuf[b]
        kx[b * tok : (b + 1) * tok, HD : 2 * HD] = bias(b * tok + iota((tok, 1), 0) < suffix_limit, tok)
        vt[:, b * tok : (b + 1) * tok] = vbuf[b].astype(F32).T.astype(BF16)
    causal = jnp.where(iota((tok, rows), 0) <= lax.rem(iota((tok, rows), 1), tok), 0.0, NEG)
    for b in range(nb):
        count = (b + 1) * tok
        qb = queries(b)
        scores = nt(kx[0:count, :], qb)
        near = scores[count - tok :] + causal
        scores = near if b == 0 else jnp.concatenate([scores[: count - tok], near], axis=0)
        top = jnp.max(scores, axis=0, keepdims=True) * rate2
        weights = jnp.exp2(scores * rate2 - top)
        mbuf[b] = top
        lbuf[b] = jnp.sum(weights, axis=0, keepdims=True)
        accbuf[b] = nn(vt[:, 0:count], weights.astype(BF16))

    pl.when(j >= 2)(chain)
    ssm_store = pltpu.make_async_copy(ybuf, ssm_o, loc.at[7])
    ssm_store.start()

    phases = phases_of(lanes, cap)
    arrived = 0
    for low, high, have in phases:
        last = high == lanes
        for c in range(arrived, have // CHUNK):
            each(lambda d: page_copy(d, c).wait_recv(), 1, n)
        arrived = have // CHUNK
        pages = high - low
        table = jnp.concatenate([own_wants] + [p[0:have] for p in places], axis=0)
        pick = nt(sorting[low:high], table).astype(BF16)
        for i in range(2 * PAGE * HD // part):
            at = slice(i * part, (i + 1) * part)
            got = recv[1:n, 0:have, at].reshape((n - 1) * have, part)
            out = nn(pick, jnp.concatenate([pmat[:, at], got], axis=0))
            for k in range(2):
                row = 2 * i + k
                piece = out[:, k * HD : (k + 1) * HD]
                if row < PAGE:
                    kx[row * pages : (row + 1) * pages, 0:HD] = piece.astype(BF16)
                    kx[row * pages : (row + 1) * pages, HD : 2 * HD] = bias(first_row[low:high] + row < prefix_limit, pages)
                else:
                    vstage[(row - PAGE) * pages : (row - PAGE + 1) * pages, :] = piece
        count = PAGE * pages
        for i in range(count // HD):
            vt[:, i * HD : (i + 1) * HD] = vstage[i * HD : (i + 1) * HD, :].T.astype(BF16)

        def block(e, carry, count=count, last=last):
            b = bpeer(e)
            scores = nt(kx[0:count, :], queries(b))
            old = mbuf[b]
            top = jnp.maximum(jnp.max(scores, axis=0, keepdims=True) * rate2, old)
            weights = jnp.exp2(scores * rate2 - top)
            factor = jnp.exp2(old - top)
            total = jnp.sum(weights, axis=0, keepdims=True) + lbuf[b] * factor
            mixed = nn(vt[:, 0:count], weights.astype(BF16)) + accbuf[b] * factor
            if not last:
                mbuf[b] = top
                lbuf[b] = total
                accbuf[b] = mixed
            else:
                alive = b * tok + lax.rem(iota((1, rows), 1), tok) < suffix_limit
                final = mixed * jnp.where(alive, 1.0 / total, 0.0)
                for h in range(GROUP):
                    obuf[b, :, h * HD : (h + 1) * HD] = final[:, h * tok : (h + 1) * tok].T.astype(BF16)

                @pl.when(e < nb)
                def _():
                    out_copy(e).start()
            return carry

        lax.fori_loop(1, nb + 1, block, 0)

    own_store = pltpu.make_async_copy(obuf.at[j], attn_o.at[:, cols(j * width, width)], loc.at[8])
    own_store.start()
    each_code(lambda k: code_copy(k).wait_send())
    each(lambda e: (q_copy(e).wait_send(), k_copy(e).wait_send(), v_copy(e).wait_send()), 1, nb)
    for c in range(chunks):
        each(lambda d: page_copy(d, c).wait_send(), 1, n)

    @pl.when(j < nb - 1)
    def _():
        state_copy().wait_send()

    ssm_store.wait()
    own_store.wait()
    each(lambda e: out_copy(e).wait(), 1, nb)


def hand_over(attn_i, ssm_i, attn_o, ssm_o, sems):
    pieces = sems.shape[0] // 2
    size = attn_i.shape[0] // pieces
    copies = []
    for k, (src, dst) in enumerate([(attn_i, attn_o), (ssm_i, ssm_o)]):
        for p in range(pieces):
            at = pl.ds(p * size, size)
            copies.append(pltpu.make_async_copy(src.at[at], dst.at[at], sems.at[k * pieces + p]))
    for copy in copies:
        copy.start()
    for copy in copies:
        copy.wait()


def local(
    queries, kv_new, page_pool, page_owner, page_slot, prefix_len, suffix_len,
    ssm_in, b_in, c_in, step_size, decay_rate, skip_gain, prior_state,
):
    n = lax.axis_size("cache")
    nb = lax.axis_size("blk")
    tok = queries.shape[1]
    lists = page_owner.shape[2]
    lanes = nb * lists
    cap = max(16, max(2, 2 * lists // n) * nb)
    spots = page_pool.shape[1]
    spread_spots = max(spots, 128)
    vmem = pl.BlockSpec(memory_space=pltpu.VMEM)
    smem = pl.BlockSpec(memory_space=pltpu.SMEM)
    hbm = pl.BlockSpec(memory_space=pl.ANY)
    dma = pltpu.SemaphoreType.DMA
    wide = SH * HP
    rows = GROUP * tok
    most = max([nb * tok] + [PAGE * (high - low) for low, high, _ in phases_of(lanes, cap)])
    chunks = cap // CHUNK
    results = (
        jax.ShapeDtypeStruct((tok, QH * HD), BF16),
        jax.ShapeDtypeStruct((tok, wide), BF16),
    )
    attn, ssm = pl.pallas_call(
        functools.partial(kernel, n, nb, cap, lists, spots),
        out_shape=results,
        in_specs=[smem, smem, vmem, vmem, hbm, hbm, hbm, hbm, vmem, vmem, vmem, vmem, vmem, hbm],
        out_specs=(hbm, hbm),
        scratch_shapes=[
            pltpu.VMEM((8, lanes), jnp.int32),
            pltpu.VMEM((n, nb, 8, lanes), jnp.int32),
            pltpu.VMEM((2, spots * PAGE, HD), BF16),
            pltpu.VMEM((spots * PAGE, HD), F32),
            pltpu.VMEM((spots * PAGE, HD), F32),
            pltpu.VMEM((spread_spots, 2 * PAGE * HD), BF16),
            pltpu.VMEM((n, cap, 2 * PAGE * HD), BF16),
            pltpu.VMEM((n, cap, 2 * PAGE * HD), BF16),
            pltpu.VMEM((nb, tok, GROUP * HD), BF16),
            pltpu.VMEM((nb, tok, HD), BF16),
            pltpu.VMEM((nb, tok, HD), BF16),
            pltpu.VMEM((most, 2 * HD), BF16),
            pltpu.VMEM((most, HD), F32),
            pltpu.VMEM((HD, most), BF16),
            pltpu.VMEM((nb, 1, rows), F32),
            pltpu.VMEM((nb, 1, rows), F32),
            pltpu.VMEM((nb, HD, rows), F32),
            pltpu.VMEM((nb, tok, GROUP * HD), BF16),
            pltpu.VMEM((tok, wide), BF16),
            pltpu.VMEM((wide, NS), F32),
            pltpu.VMEM((tok, wide), F32),
            pltpu.VMEM((8, wide), F32),
            pltpu.VMEM((tok, wide), BF16),
            pltpu.VMEM((NS, wide), F32),
            pltpu.VMEM((tok, wide), BF16),
            pltpu.VMEM((NS, wide), BF16),
            pltpu.VMEM((NS, wide), BF16),
            dma((9,)), dma((n * nb,)), dma((n * nb,)), dma((n, chunks)), dma((n, chunks)),
            dma((nb,)), dma((nb,)), dma((nb,)), dma((nb,)), dma((nb,)), dma((nb,)),
            dma((nb,)), dma((nb,)), dma, dma,
        ],
        compiler_params=pltpu.CompilerParams(
            collective_id=0, has_side_effects=True, vmem_limit_bytes=56 * 1024 * 1024
        ),
    )(
        prefix_len, suffix_len, page_owner[0, 0, :, 0][None], page_slot[0], queries[0], kv_new[0],
        page_pool.reshape(spots * PAGE, 2 * KVH * HD), ssm_in[0], b_in[0], c_in[0], step_size[0].T,
        decay_rate[None, :], skip_gain[None, :], prior_state.reshape(wide, NS),
    )
    attn, ssm = pl.pallas_call(
        hand_over,
        out_shape=results,
        in_specs=[hbm, hbm],
        out_specs=(hbm, hbm),
        scratch_shapes=[dma((8,))],
    )(attn, ssm)
    return attn[None], ssm[None]


def solution(mesh):
    in_specs = (
        P(("groups", "cache"), "blk", None),
        P(("groups", "cache"), "blk", None),
        P(("groups", "cache"), None, None, None),
        P(("groups", "cache"), "blk", None, None),
        P(("groups", "cache"), "blk", None),
        P(("groups", "cache")),
        P(("groups", "cache")),
        P(("groups", "cache"), "blk", None),
        P(("groups", "cache"), "blk", None),
        P(("groups", "cache"), "blk", None),
        P(("groups", "cache"), "blk", None),
        P(),
        P(),
        P(("groups", "cache"), None, None, None),
    )
    out_specs = (P(("groups", "cache"), "blk", None), P(("groups", "cache"), "blk", None))
    return jax.shard_map(local, mesh=mesh, in_specs=in_specs, out_specs=out_specs, check_vma=False)
```

time: 76.8 us -> 83.6 us (1.089)
  the two profiles are of different devices: /device:TPU:21 before, /device:TPU:9 now
where the time goes in v1:
time: 83.6 us; the launch traced here: 82.9 us
  Pallas kernels  80.9 us (97%)
  between operations  1.93 us (2%)
    pallas_call x1, Pallas kernels, local(): pl.pallas_call(functools.partial(kernel, n, nb, cap, lists, spots), out_s...  48 us
    pallas_call x1, Pallas kernels, local(): pl.pallas_call(hand_over, out_shape=results, in_specs=[hbm, hbm], out_spe...  32.9 us

profile of v1, /device:TPU:9, one launch (start us, length us, event | category | flops | bytes accessed | tf_op | source)
XLA Modules:
  0.0 82.9 jit_solution(4691479508364060463)
XLA Ops:
  1.9 48.0 %shard_map.149 = (bf16[128,2048]{1,0:T(8,128)(2,1)}, bf16[128,2048]{1,0:T(8,128)(2,1)}) custom-call(s32[1]{0:T(128)S(6)} %copy.16.plen, s32[1]{0:T(128)S(6)} %copy.17.slen, s32[1,32]{1,0:T(1,128)} %bitcast.24, s32[1,32]{1,0:T(1,128)} %bitcast.25, bf16[128,2048]{1,0:T(8,128)(2,1)} %bitcast.18, bf16[128,1024]{1,0:T(8,128)(2,1)} %bitcast.20, ...), custom_call_target="tpu_custom_call" | custom-call | tf_op jit(solution)/shard_map/pallas_call | solution.py:465
  49.9 32.9 %shard_map.150 = (bf16[128,2048]{1,0:T(8,128)(2,1)}, bf16[128,2048]{1,0:T(8,128)(2,1)}) custom-call(bf16[128,2048]{1,0:T(8,128)(2,1)} %get-tuple-element.6.attn_i, bf16[128,2048]{1,0:T(8,128)(2,1)} %get-tuple-element.7.ssm_i), custom_call_target="tpu_custom_call" | custom-call | tf_op jit(solution)/shard_map/pallas_call | solution.py:510

commit v2 on v1

--- a/solution.py
+++ b/solution.py
@@ -425,13 +425,13 @@
 
 
 def hand_over(attn_i, ssm_i, attn_o, ssm_o, sems):
-    pieces = sems.shape[0] // 2
+    pieces = sems.shape[1] // 2
     size = attn_i.shape[0] // pieces
     copies = []
     for k, (src, dst) in enumerate([(attn_i, attn_o), (ssm_i, ssm_o)]):
         for p in range(pieces):
             at = pl.ds(p * size, size)
-            copies.append(pltpu.make_async_copy(src.at[at], dst.at[at], sems.at[k * pieces + p]))
+            copies.append(pltpu.make_async_copy(src.at[at], dst.at[at], sems.at[0, k * pieces + p]))
     for copy in copies:
         copy.start()
     for copy in copies:
@@ -511,8 +511,8 @@
         hand_over,
         out_shape=results,
         in_specs=[hbm, hbm],
-        out_specs=(hbm, hbm),
-        scratch_shapes=[dma((8,))],
+        out_specs=(vmem, vmem),
+        scratch_shapes=[dma((1, 4))],
     )(attn, ssm)
     return attn[None], ssm[None]
 

time: 83.6 us -> 52.8 us (0.63)
  Pallas kernels: 80.9 us -> 50.2 us
    pallas_call x1, Pallas kernels: 32.9 us -> 2.19 us  [local(): pl.pallas_call(hand_over, out_shape=results, in_specs=[hbm, hbm], out_spe...]
where the time goes in v2:
time: 52.8 us; the launch traced here: 52.1 us
  Pallas kernels  50.2 us (95%)
  between operations  1.93 us (4%)
    pallas_call x1, Pallas kernels, local(): pl.pallas_call(functools.partial(kernel, n, nb, cap, lists, spots), out_s...  48 us
    pallas_call x1, Pallas kernels, local(): pl.pallas_call(hand_over, out_shape=results, in_specs=[hbm, hbm], out_spe...  2.19 us

profile of v2, /device:TPU:9, one launch (start us, length us, event | category | flops | bytes accessed | tf_op | source)
XLA Modules:
  0.0 52.1 jit_solution(717908625324286678)
XLA Ops:
  1.9 48.0 %shard_map.149 = (bf16[128,2048]{1,0:T(8,128)(2,1)}, bf16[128,2048]{1,0:T(8,128)(2,1)}) custom-call(s32[1]{0:T(128)S(6)} %copy.16.plen, s32[1]{0:T(128)S(6)} %copy.17.slen, s32[1,32]{1,0:T(1,128)} %bitcast.24, s32[1,32]{1,0:T(1,128)} %bitcast.25, bf16[128,2048]{1,0:T(8,128)(2,1)} %bitcast.18, bf16[128,1024]{1,0:T(8,128)(2,1)} %bitcast.20, ...), custom_call_target="tpu_custom_call" | custom-call | tf_op jit(solution)/shard_map/pallas_call | solution.py:465
  49.9 2.2 %shard_map.150 = (bf16[128,2048]{1,0:T(8,128)(2,1)}, bf16[128,2048]{1,0:T(8,128)(2,1)}) custom-call(bf16[128,2048]{1,0:T(8,128)(2,1)} %get-tuple-element.6.attn_i, bf16[128,2048]{1,0:T(8,128)(2,1)} %get-tuple-element.7.ssm_i), custom_call_target="tpu_custom_call" | custom-call | tf_op jit(solution)/shard_map/pallas_call | solution.py:510

commit v3 on v2

--- a/solution.py
+++ b/solution.py
@@ -70,7 +70,7 @@
     plen, slen, owner, slot, q, kv, pool, x_hbm, b_rows, c_rows, dt_t, rate, skip, prior_hbm,
     attn_o, ssm_o,
     code, codes, praw, pf_k, pf_v, pmat, sendbuf, recv, qbuf, kbuf, vbuf, kx, vstage, vt, mbuf, lbuf, accbuf, obuf,
-    x, prior, afull, skipf, xp, sbuf, ybuf, hin, hout,
+    x, prior, afull, skipf, xp, sbuf, hin, hout,
     loc, cs, cr, ps, pr, qs, qr, ks, kr, vs, vr, os, orr, hs, hr,
 ):
     me = lax.axis_index("cache")
@@ -106,11 +106,15 @@
     barrier = pltpu.get_barrier_semaphore()
 
     def greet(k, carry):
-        peer = {"cache": zpeer(k // nb), "blk": bpeer(lax.rem(k, nb))}
+        peer = {"cache": zpeer(k // nb), "blk": bpeer(k % nb)}
         pl.semaphore_signal(barrier, inc=1, device_id=peer, device_id_type=pl.DeviceIdType.MESH)
         return carry
 
-    lax.fori_loop(1, n * nb, greet, 0)
+    if n * nb <= 16:
+        for k in range(1, n * nb):
+            greet(k, 0)
+    else:
+        lax.fori_loop(1, n * nb, greet, 0)
     for load in loads:
         load.start()
 
@@ -119,10 +123,68 @@
         prior_load.start()
 
     mine = iota((1, lanes), 1) // lists == j
-    code[...] = jnp.zeros_like(code)
-    code[0:1, :] = jnp.where(mine, jnp.concatenate([owner[...]] * nb, axis=1) + 1, 0)
-    code[1:2, :] = jnp.where(mine, jnp.concatenate([slot[...]] * nb, axis=1), 0)
+    named_slots = slot[...] * n + owner[...]
+    code[...] = jnp.where(mine, jnp.concatenate([named_slots] * nb, axis=1), 0)
     codes[me, j] = code[...]
+
+    pl.semaphore_wait(barrier, n * nb - 1)
+
+    def code_copy(k):
+        peer = {"cache": zpeer(k // nb), "blk": bpeer(k % nb)}
+        return remote(code, codes.at[me, j], cs.at[k], cr.at[k], peer)
+
+    def q_copy(e):
+        to = bpeer(e)
+        return remote(q.at[:, cols(to * width, width)], qbuf.at[j], qs.at[e], qr.at[e], {"blk": to})
+
+    def k_copy(e):
+        to = bpeer(e)
+        return remote(kv.at[:, cols(to * HD, HD)], kbuf.at[j], ks.at[e], kr.at[e], {"blk": to})
+
+    def v_copy(e):
+        to = bpeer(e)
+        return remote(kv.at[:, cols(half + to * HD, HD)], vbuf.at[j], vs.at[e], vr.at[e], {"blk": to})
+
+    def page_copy(d, c):
+        at = pl.ds(c * CHUNK, CHUNK)
+        return remote(sendbuf.at[d, at], recv.at[d, at], ps.at[d, c], pr.at[d, c], {"cache": zpeer(d)})
+
+    def state_copy():
+        return remote(hout, hin, hs, hr, {"blk": bpeer(1)})
+
+    def out_copy(e):
+        to = bpeer(e)
+        return remote(obuf.at[to], attn_o.at[:, cols(j * width, width)], os.at[e], orr.at[e], {"blk": to})
+
+    def each(what, low, high):
+        if high - low <= 16:
+            for i in range(low, high):
+                what(i)
+            return
+
+        def body(i, carry):
+            what(i)
+            return carry
+
+        lax.fori_loop(low, high, body, 0)
+
+    def each_code(what):
+        each(what, 1, n * nb)
+
+    each_code(lambda k: code_copy(k).start())
+
+    each(lambda e: (k_copy(e).start(), v_copy(e).start(), q_copy(e).start()), 1, nb)
+
+    loads[1].wait()
+    loads[2].wait()
+    pf_k[...] = praw[0].astype(F32)
+    pf_v[...] = praw[1].astype(F32)
+    if spots < pmat.shape[0]:
+        pmat[...] = jnp.zeros_like(pmat)
+    for i in range(PAGE):
+        at = pl.ds(i, spots, stride=PAGE)
+        pmat[0:spots, i * HD : (i + 1) * HD] = pf_k[at, :].astype(BF16)
+        pmat[0:spots, (PAGE + i) * HD : (PAGE + i + 1) * HD] = pf_v[at, :].astype(BF16)
 
     dt = dt_t[...].T
     fall = jnp.concatenate(thirds(dt * (-rate[...])), axis=0).astype(BF16)
@@ -159,6 +221,36 @@
         hout[:, at] = (afull[tok - 1 : tok, at] * (hin[:, at].astype(F32) + sbuf[:, at])).astype(BF16)
         return carry
 
+    before = jnp.where(iota((lanes, lanes), 0) < iota((lanes, lanes), 1), 1.0, 0.0).astype(BF16)
+
+    def comb(r):
+        both = jnp.sum(codes[r], axis=0)
+        return lax.rem(both, n), both // n
+
+    def ranked(named):
+        flags = jnp.broadcast_to(jnp.where(named, 1.0, 0.0), (16, lanes)).astype(BF16)
+        return nn(flags, before)[0:1].astype(jnp.int32)
+
+    def onehot(flag):
+        return jnp.where(flag, 1.0, 0.0).astype(BF16)
+
+    each_code(lambda k: code_copy(k).wait_recv())
+    spread_spots = pmat.shape[0]
+
+    def answer(d):
+        owners, slots = comb(zpeer(d))
+        named = owners == me
+        place = onehot((ranked(named) == iota((cap, lanes), 0)) & named)
+        wants = onehot(slots == iota((spread_spots, lanes), 0))
+        chosen = nt(place, wants).astype(BF16)
+        for i in range(2 * PAGE * HD // part):
+            sendbuf[d, :, i * part : (i + 1) * part] = nn(chosen, pmat[:, i * part : (i + 1) * part]).astype(BF16)
+        page_copy(d, 0).start()
+
+    each(answer, 1, n)
+    for c in range(1, chunks):
+        each(lambda d: page_copy(d, c).start(), 1, n)
+
     @pl.when(j == 0)
     def _():
         prior_load.wait()
@@ -170,105 +262,10 @@
 
         lax.fori_loop(0, wide // HD, fill, 0)
         lax.fori_loop(0, parts, onward, 0)
-
-    loads[1].wait()
-    loads[2].wait()
-    pf_k[...] = praw[0].astype(F32)
-    pf_v[...] = praw[1].astype(F32)
-    if spots < pmat.shape[0]:
-        pmat[...] = jnp.zeros_like(pmat)
-    for i in range(PAGE):
-        at = pl.ds(i, spots, stride=PAGE)
-        pmat[0:spots, i * HD : (i + 1) * HD] = pf_k[at, :].astype(BF16)
-        pmat[0:spots, (PAGE + i) * HD : (PAGE + i + 1) * HD] = pf_v[at, :].astype(BF16)
-
-    pl.semaphore_wait(barrier, n * nb - 1)
-
-    def code_copy(k):
-        peer = {"cache": zpeer(k // nb), "blk": bpeer(lax.rem(k, nb))}
-        return remote(code, codes.at[me, j], cs.at[k], cr.at[k], peer)
-
-    def q_copy(e):
-        to = bpeer(e)
-        return remote(q.at[:, cols(to * width, width)], qbuf.at[j], qs.at[e], qr.at[e], {"blk": to})
-
-    def k_copy(e):
-        to = bpeer(e)
-        return remote(kv.at[:, cols(to * HD, HD)], kbuf.at[j], ks.at[e], kr.at[e], {"blk": to})
-
-    def v_copy(e):
-        to = bpeer(e)
-        return remote(kv.at[:, cols(half + to * HD, HD)], vbuf.at[j], vs.at[e], vr.at[e], {"blk": to})
-
-    def page_copy(d, c):
-        at = pl.ds(c * CHUNK, CHUNK)
-        return remote(sendbuf.at[d, at], recv.at[d, at], ps.at[d, c], pr.at[d, c], {"cache": zpeer(d)})
-
-    def state_copy():
-        return remote(hout, hin, hs, hr, {"blk": bpeer(1)})
-
-    def out_copy(e):
-        to = bpeer(e)
-        return remote(obuf.at[to], attn_o.at[:, cols(j * width, width)], os.at[e], orr.at[e], {"blk": to})
-
-    def each(what, low, high):
-        if high - low <= 4:
-            for i in range(low, high):
-                what(i)
-            return
-
-        def body(i, carry):
-            what(i)
-            return carry
-
-        lax.fori_loop(low, high, body, 0)
-
-    def each_code(what):
-        def body(k, carry):
-            what(k)
-            return carry
-
-        lax.fori_loop(1, n * nb, body, 0)
-
-    each_code(lambda k: code_copy(k).start())
-
-    @pl.when(j == 0)
-    def _():
         state_copy().start()
 
-    each(lambda e: (k_copy(e).start(), v_copy(e).start(), q_copy(e).start()), 1, nb)
-
-    before = jnp.where(iota((lanes, lanes), 0) < iota((lanes, lanes), 1), 1.0, 0.0).astype(BF16)
-
-    def comb(r):
-        return jnp.sum(codes[r], axis=0)
-
-    def ranked(named):
-        flags = jnp.broadcast_to(jnp.where(named, 1.0, 0.0), (16, lanes)).astype(BF16)
-        return nn(flags, before)[0:1].astype(jnp.int32)
-
-    def onehot(flag):
-        return jnp.where(flag, 1.0, 0.0).astype(BF16)
-
-    each_code(lambda k: code_copy(k).wait_recv())
-    spread_spots = pmat.shape[0]
-
-    def answer(d):
-        pair = comb(zpeer(d))
-        named = pair[0:1] == me + 1
-        place = onehot((ranked(named) == iota((cap, lanes), 0)) & named)
-        wants = onehot(pair[1:2] == iota((spread_spots, lanes), 0))
-        chosen = nt(place, wants).astype(BF16)
-        for i in range(2 * PAGE * HD // part):
-            sendbuf[d, :, i * part : (i + 1) * part] = nn(chosen, pmat[:, i * part : (i + 1) * part]).astype(BF16)
-        page_copy(d, 0).start()
-
-    each(answer, 1, n)
-    for c in range(1, chunks):
-        each(lambda d: page_copy(d, c).start(), 1, n)
-
-    pair = comb(me)
-    back = me + 1 - pair[0:1]
+    owners, slots = comb(me)
+    back = me - owners
     away = jnp.where(back < 0, back + n, back)
     rank = jnp.zeros((1, lanes), jnp.int32)
 
@@ -291,7 +288,7 @@
     sorting = sorted_f.astype(BF16)
     number = (lax.rem(lane, lists) * nb + lane // lists).astype(F32)
     first_row = jnp.sum(sorted_f * number, axis=1, keepdims=True).astype(jnp.int32) * PAGE
-    own_wants = onehot((pair[1:2] == iota((spread_spots, lanes), 0)) & (away == 0))
+    own_wants = onehot((slots == iota((spread_spots, lanes), 0)) & (away == 0))
     places = [onehot((rank == iota((cap, lanes), 0)) & (away == d)) for d in range(1, n)]
 
     def read_block():
@@ -301,7 +298,7 @@
             at = cols(i * part, part)
             both = jnp.concatenate([xp[:, at], hin[:, at]], axis=0)
             total = afull[:, at] * nn(readout, both) + skipf[0:1, at] * x[:, at].astype(F32)
-            ybuf[:, at] = jnp.where(alive, total, 0.0).astype(BF16)
+            ssm_o[:, at] = jnp.where(alive, total, 0.0).astype(BF16)
             return carry
 
         lax.fori_loop(0, parts, body, 0)
@@ -353,19 +350,24 @@
         accbuf[b] = nn(vt[:, 0:count], weights.astype(BF16))
 
     pl.when(j >= 2)(chain)
-    ssm_store = pltpu.make_async_copy(ybuf, ssm_o, loc.at[7])
-    ssm_store.start()
 
     phases = phases_of(lanes, cap)
     arrived = 0
+    picks = []
     for low, high, have in phases:
+        table = jnp.concatenate([own_wants] + [p[0:have] for p in places], axis=0)
+        picks.append(nt(sorting[low:high], table).astype(BF16))
+    if nb == 4:
+        over = 1 + 2 * lax.rem(j + 1, 2)
+        order = [2, over, nb - over, nb]
+    else:
+        order = list(range(1, nb + 1))
+    for pick, (low, high, have) in zip(picks, phases):
         last = high == lanes
         for c in range(arrived, have // CHUNK):
             each(lambda d: page_copy(d, c).wait_recv(), 1, n)
         arrived = have // CHUNK
         pages = high - low
-        table = jnp.concatenate([own_wants] + [p[0:have] for p in places], axis=0)
-        pick = nt(sorting[low:high], table).astype(BF16)
         for i in range(2 * PAGE * HD // part):
             at = slice(i * part, (i + 1) * part)
             got = recv[1:n, 0:have, at].reshape((n - 1) * have, part)
@@ -382,7 +384,7 @@
         for i in range(count // HD):
             vt[:, i * HD : (i + 1) * HD] = vstage[i * HD : (i + 1) * HD, :].T.astype(BF16)
 
-        def block(e, carry, count=count, last=last):
+        for turn, e in enumerate(order):
             b = bpeer(e)
             scores = nt(kx[0:count, :], queries(b))
             old = mbuf[b]
@@ -398,18 +400,14 @@
             else:
                 alive = b * tok + lax.rem(iota((1, rows), 1), tok) < suffix_limit
                 final = mixed * jnp.where(alive, 1.0 / total, 0.0)
-                for h in range(GROUP):
-                    obuf[b, :, h * HD : (h + 1) * HD] = final[:, h * tok : (h + 1) * tok].T.astype(BF16)
-
-                @pl.when(e < nb)
-                def _():
+                heads = [final[:, h * tok : (h + 1) * tok].T.astype(BF16) for h in range(GROUP)]
+                result = jnp.concatenate(heads, axis=1)
+                if turn < nb - 1:
+                    obuf[b] = result
                     out_copy(e).start()
-            return carry
-
-        lax.fori_loop(1, nb + 1, block, 0)
-
-    own_store = pltpu.make_async_copy(obuf.at[j], attn_o.at[:, cols(j * width, width)], loc.at[8])
-    own_store.start()
+                else:
+                    attn_o[:, cols(j * width, width)] = result
+
     each_code(lambda k: code_copy(k).wait_send())
     each(lambda e: (q_copy(e).wait_send(), k_copy(e).wait_send(), v_copy(e).wait_send()), 1, nb)
     for c in range(chunks):
@@ -419,23 +417,7 @@
     def _():
         state_copy().wait_send()
 
-    ssm_store.wait()
-    own_store.wait()
     each(lambda e: out_copy(e).wait(), 1, nb)
-
-
-def hand_over(attn_i, ssm_i, attn_o, ssm_o, sems):
-    pieces = sems.shape[1] // 2
-    size = attn_i.shape[0] // pieces
-    copies = []
-    for k, (src, dst) in enumerate([(attn_i, attn_o), (ssm_i, ssm_o)]):
-        for p in range(pieces):
-            at = pl.ds(p * size, size)
-            copies.append(pltpu.make_async_copy(src.at[at], dst.at[at], sems.at[0, k * pieces + p]))
-    for copy in copies:
-        copy.start()
-    for copy in copies:
-        copy.wait()
 
 
 def local(
@@ -452,7 +434,7 @@
     spread_spots = max(spots, 128)
     vmem = pl.BlockSpec(memory_space=pltpu.VMEM)
     smem = pl.BlockSpec(memory_space=pltpu.SMEM)
-    hbm = pl.BlockSpec(memory_space=pl.ANY)
+    hbm = pl.BlockSpec(memory_space=pltpu.HBM)
     dma = pltpu.SemaphoreType.DMA
     wide = SH * HP
     rows = GROUP * tok
@@ -464,12 +446,12 @@
     )
     attn, ssm = pl.pallas_call(
         functools.partial(kernel, n, nb, cap, lists, spots),
-        out_shape=results,
+        out_shape=tuple(pltpu.VMEM(r.shape, r.dtype) for r in results),
         in_specs=[smem, smem, vmem, vmem, hbm, hbm, hbm, hbm, vmem, vmem, vmem, vmem, vmem, hbm],
-        out_specs=(hbm, hbm),
+        out_specs=(vmem, vmem),
         scratch_shapes=[
-            pltpu.VMEM((8, lanes), jnp.int32),
-            pltpu.VMEM((n, nb, 8, lanes), jnp.int32),
+            pltpu.VMEM((1, lanes), jnp.int32),
+            pltpu.VMEM((n, nb, 1, lanes), jnp.int32),
             pltpu.VMEM((2, spots * PAGE, HD), BF16),
             pltpu.VMEM((spots * PAGE, HD), F32),
             pltpu.VMEM((spots * PAGE, HD), F32),
@@ -492,10 +474,9 @@
             pltpu.VMEM((8, wide), F32),
             pltpu.VMEM((tok, wide), BF16),
             pltpu.VMEM((NS, wide), F32),
-            pltpu.VMEM((tok, wide), BF16),
             pltpu.VMEM((NS, wide), BF16),
             pltpu.VMEM((NS, wide), BF16),
-            dma((9,)), dma((n * nb,)), dma((n * nb,)), dma((n, chunks)), dma((n, chunks)),
+            dma((7,)), dma((n * nb,)), dma((n * nb,)), dma((n, chunks)), dma((n, chunks)),
             dma((nb,)), dma((nb,)), dma((nb,)), dma((nb,)), dma((nb,)), dma((nb,)),
             dma((nb,)), dma((nb,)), dma, dma,
         ],
@@ -507,13 +488,6 @@
         page_pool.reshape(spots * PAGE, 2 * KVH * HD), ssm_in[0], b_in[0], c_in[0], step_size[0].T,
         decay_rate[None, :], skip_gain[None, :], prior_state.reshape(wide, NS),
     )
-    attn, ssm = pl.pallas_call(
-        hand_over,
-        out_shape=results,
-        in_specs=[hbm, hbm],
-        out_specs=(vmem, vmem),
-        scratch_shapes=[dma((1, 4))],
-    )(attn, ssm)
     return attn[None], ssm[None]
 
 

time: 52.8 us -> 47.2 us (0.89)
  Pallas kernels: 50.2 us -> 43 us
  local copies, waits for them, and re-layouts: 0 us -> 1.59 us
    pallas_call x1, Pallas kernels: 48 us -> 43 us  [local(): pl.pallas_call(functools.partial(kernel, n, nb, cap, lists, spots), out_s...]
    pallas_call x1 -> x0, Pallas kernels: 2.19 us -> none  [local(): pl.pallas_call(hand_over, out_shape=results, in_specs=[hbm, hbm], out_spe...]
    unnamed x0 -> x2, local copies, waits for them, and re-layouts: none -> 1.59 us
where the time goes in v3:
time: 47.2 us; the launch traced here: 46.5 us
  Pallas kernels  43 us (91%)
  between operations  1.93 us (4%)
  local copies, waits for them, and re-layouts  1.59 us (3%)
    pallas_call x1, Pallas kernels, local(): pl.pallas_call(functools.partial(kernel, n, nb, cap, lists, spots), out_s...  43 us
    unnamed x2, local copies, waits for them, and re-layouts  1.59 us

profile of v3, /device:TPU:9, one launch (start us, length us, event | category | flops | bytes accessed | tf_op | source)
XLA Modules:
  0.0 46.5 jit_solution(18006551137978885551)
XLA Ops:
  1.9 43.0 %shard_map.149 = (bf16[128,2048]{1,0:T(8,128)(2,1)S(1)}, bf16[128,2048]{1,0:T(8,128)(2,1)S(1)}) custom-call(s32[1]{0:T(128)S(6)} %copy.20.plen, s32[1]{0:T(128)S(6)} %copy.21.slen, s32[1,32]{1,0:T(1,128)} %bitcast.26, s32[1,32]{1,0:T(1,128)} %bitcast.27, bf16[128,2048]{1,0:T(8,128)(2,1)} %bitcast.20, bf16[128,1024]{1,0:T(8,128)(2,1)} %bitcast.22, ...), custom_call_target="tpu_custom_call" | custom-call | tf_op jit(solution)/shard_map/pallas_call | solution.py:447
  44.9 0.8 %copy.18 = bf16[1,128,2048]{2,1,0:T(8,128)(2,1)} copy(bf16[1,128,2048]{2,1,0:T(8,128)(2,1)S(1)} %bitcast.17) | data formatting | bytes 1048576
  45.7 0.8 %copy.19 = bf16[1,128,2048]{2,1,0:T(8,128)(2,1)} copy(bf16[1,128,2048]{2,1,0:T(8,128)(2,1)S(1)} %bitcast.16) | data formatting | bytes 1048576

commit v4 on v3

--- a/solution.py
+++ b/solution.py
@@ -17,7 +17,8 @@
 PAGE = 8
 GROUP = QH // KVH
 NEG = -1e30
-CHUNK = 16
+PIECES = 2
+PD = HD // PIECES
 F32 = jnp.float32
 BF16 = jnp.bfloat16
 
@@ -52,24 +53,11 @@
     return [hi, mid, (rest - mid).astype(BF16).astype(F32)]
 
 
-def phases_of(total, cap):
-    found, done = [], 0
-    for have in [cap - CHUNK, cap]:
-        if have <= 0:
-            continue
-        late = total // cap * (cap - have) + max(total % cap - have, 0)
-        ready = (total - late) // 16 * 16
-        if ready > done:
-            found.append((done, ready, have))
-            done = ready
-    return found
-
-
 def kernel(
     n, nb, cap, lists, spots,
     plen, slen, owner, slot, q, kv, pool, x_hbm, b_rows, c_rows, dt_t, rate, skip, prior_hbm,
     attn_o, ssm_o,
-    code, codes, praw, pf_k, pf_v, pmat, sendbuf, recv, qbuf, kbuf, vbuf, kx, vstage, vt, mbuf, lbuf, accbuf, obuf,
+    code, codes, praw, pf_k, pf_v, pmat, sendbuf, recv, qbuf, kbuf, vbuf, kx, vt, vpart, mbuf, lbuf, accbuf, wbuf, obuf, ostage,
     x, prior, afull, skipf, xp, sbuf, hin, hout,
     loc, cs, cr, ps, pr, qs, qr, ks, kr, vs, vr, os, orr, hs, hr,
 ):
@@ -83,7 +71,8 @@
     rows = GROUP * tok
     prefix_limit = plen[0]
     suffix_limit = slen[0]
-    chunks = cap // CHUNK
+    part = 2 * HD
+    parts = wide // part
 
     def zpeer(d):
         return lax.rem(me + d, n)
@@ -95,9 +84,9 @@
         return pl.ds(pl.multiple_of(at, 128), size)
 
     loads = [
-        pltpu.make_async_copy(x_hbm, x, loc.at[0]),
-        pltpu.make_async_copy(pool.at[:, cols(j * HD, HD)], praw.at[0], loc.at[1]),
-        pltpu.make_async_copy(pool.at[:, cols(half + j * HD, HD)], praw.at[1], loc.at[2]),
+        pltpu.make_async_copy(pool.at[:, cols(j * HD, HD)], praw.at[0], loc.at[0]),
+        pltpu.make_async_copy(pool.at[:, cols(half + j * HD, HD)], praw.at[1], loc.at[1]),
+        pltpu.make_async_copy(x_hbm, x, loc.at[2]),
         pltpu.make_async_copy(q.at[:, cols(j * width, width)], qbuf.at[j], loc.at[3]),
         pltpu.make_async_copy(kv.at[:, cols(j * HD, HD)], kbuf.at[j], loc.at[4]),
         pltpu.make_async_copy(kv.at[:, cols(half + j * HD, HD)], vbuf.at[j], loc.at[5]),
@@ -115,13 +104,6 @@
             greet(k, 0)
     else:
         lax.fori_loop(1, n * nb, greet, 0)
-    for load in loads:
-        load.start()
-
-    @pl.when(j == 0)
-    def _():
-        prior_load.start()
-
     mine = iota((1, lanes), 1) // lists == j
     named_slots = slot[...] * n + owner[...]
     code[...] = jnp.where(mine, jnp.concatenate([named_slots] * nb, axis=1), 0)
@@ -146,15 +128,15 @@
         return remote(kv.at[:, cols(half + to * HD, HD)], vbuf.at[j], vs.at[e], vr.at[e], {"blk": to})
 
     def page_copy(d, c):
-        at = pl.ds(c * CHUNK, CHUNK)
-        return remote(sendbuf.at[d, at], recv.at[d, at], ps.at[d, c], pr.at[d, c], {"cache": zpeer(d)})
+        at = pl.ds(0, PAGE * HD) if c == 0 else pl.ds(PAGE * HD + (c - 1) * PAGE * PD, PAGE * PD)
+        return remote(sendbuf.at[d, :, at], recv.at[d, :, at], ps.at[d, c], pr.at[d, c], {"cache": zpeer(d)})
 
     def state_copy():
         return remote(hout, hin, hs, hr, {"blk": bpeer(1)})
 
-    def out_copy(e):
+    def out_copy(e, s):
         to = bpeer(e)
-        return remote(obuf.at[to], attn_o.at[:, cols(j * width, width)], os.at[e], orr.at[e], {"blk": to})
+        return remote(obuf.at[s, to], ostage.at[s, j], os.at[e, s], orr.at[e, s], {"blk": to})
 
     def each(what, low, high):
         if high - low <= 16:
@@ -172,19 +154,84 @@
         each(what, 1, n * nb)
 
     each_code(lambda k: code_copy(k).start())
-
-    each(lambda e: (k_copy(e).start(), v_copy(e).start(), q_copy(e).start()), 1, nb)
-
+    for load in loads:
+        load.start()
+
+    @pl.when(j == 0)
+    def _():
+        prior_load.start()
+
+    loads[0].wait()
     loads[1].wait()
-    loads[2].wait()
     pf_k[...] = praw[0].astype(F32)
     pf_v[...] = praw[1].astype(F32)
     if spots < pmat.shape[0]:
         pmat[...] = jnp.zeros_like(pmat)
+    values = []
     for i in range(PAGE):
         at = pl.ds(i, spots, stride=PAGE)
         pmat[0:spots, i * HD : (i + 1) * HD] = pf_k[at, :].astype(BF16)
-        pmat[0:spots, (PAGE + i) * HD : (PAGE + i + 1) * HD] = pf_v[at, :].astype(BF16)
+        values.append(pf_v[at, :])
+    for s in range(PIECES):
+        for t in range(PAGE // PIECES):
+            tile = [values[t * PIECES + k][:, s * PD : (s + 1) * PD] for k in range(PIECES)]
+            at = PAGE * HD + s * PAGE * PD + t * HD
+            pmat[0:spots, at : at + HD] = jnp.concatenate(tile, axis=1).astype(BF16)
+
+    @pl.when(j == 0)
+    def _():
+        prior_load.wait()
+
+        def fill(i, carry):
+            at = cols(i * HD, HD)
+            hin[:, at] = prior[at, :].T.astype(BF16)
+            return carry
+
+        lax.fori_loop(0, wide // HD, fill, 0)
+
+    before = jnp.where(iota((lanes, lanes), 0) < iota((lanes, lanes), 1), 1.0, 0.0).astype(BF16)
+
+    def comb(r):
+        both = jnp.sum(codes[r], axis=0)
+        return lax.rem(both, n), both // n
+
+    def ranked(named):
+        flags = jnp.broadcast_to(jnp.where(named, 1.0, 0.0), (16, lanes)).astype(BF16)
+        return nn(flags, before)[0:1].astype(jnp.int32)
+
+    def onehot(flag):
+        return jnp.where(flag, 1.0, 0.0).astype(BF16)
+
+    each_code(lambda k: code_copy(k).wait_recv())
+    spread_spots = pmat.shape[0]
+
+    def chosen_for(d):
+        owners, slots = comb(zpeer(d))
+        named = owners == me
+        place = onehot((ranked(named) == iota((cap, lanes), 0)) & named)
+        wants = onehot(slots == iota((spread_spots, lanes), 0))
+        return nt(place, wants).astype(BF16)
+
+    def answer(d, chosen, c):
+        low = 0 if c == 0 else PAGE * HD + (c - 1) * PAGE * PD
+        high = PAGE * HD + c * PAGE * PD
+        for at in range(low, high, part):
+            sendbuf[d, :, at : at + part] = nn(chosen, pmat[:, at : at + part]).astype(BF16)
+        page_copy(d, c).start()
+
+    if n <= 8:
+        wanted = [chosen_for(d) for d in range(1, n)]
+        for c in range(1 + PIECES):
+            for d in range(1, n):
+                answer(d, wanted[d - 1], c)
+    else:
+        def answer_all(d):
+            chosen = chosen_for(d)
+            for c in range(1 + PIECES):
+                answer(d, chosen, c)
+
+        each(answer_all, 1, n)
+    each(lambda e: (k_copy(e).start(), v_copy(e).start(), q_copy(e).start()), 1, nb)
 
     dt = dt_t[...].T
     fall = jnp.concatenate(thirds(dt * (-rate[...])), axis=0).astype(BF16)
@@ -197,10 +244,8 @@
     gram = jnp.where(lower, nt(c_rows[...], b_rows[...]), 0.0).astype(BF16)
     readout = jnp.concatenate([gram, c_rows[...]], axis=1)
     b_t = b_rows[...].astype(F32).T.astype(BF16)
-    part = 2 * HD
-    parts = wide // part
-
-    loads[0].wait()
+
+    loads[2].wait()
 
     def own_block(i, carry):
         at = cols(i * part, part)
@@ -221,46 +266,8 @@
         hout[:, at] = (afull[tok - 1 : tok, at] * (hin[:, at].astype(F32) + sbuf[:, at])).astype(BF16)
         return carry
 
-    before = jnp.where(iota((lanes, lanes), 0) < iota((lanes, lanes), 1), 1.0, 0.0).astype(BF16)
-
-    def comb(r):
-        both = jnp.sum(codes[r], axis=0)
-        return lax.rem(both, n), both // n
-
-    def ranked(named):
-        flags = jnp.broadcast_to(jnp.where(named, 1.0, 0.0), (16, lanes)).astype(BF16)
-        return nn(flags, before)[0:1].astype(jnp.int32)
-
-    def onehot(flag):
-        return jnp.where(flag, 1.0, 0.0).astype(BF16)
-
-    each_code(lambda k: code_copy(k).wait_recv())
-    spread_spots = pmat.shape[0]
-
-    def answer(d):
-        owners, slots = comb(zpeer(d))
-        named = owners == me
-        place = onehot((ranked(named) == iota((cap, lanes), 0)) & named)
-        wants = onehot(slots == iota((spread_spots, lanes), 0))
-        chosen = nt(place, wants).astype(BF16)
-        for i in range(2 * PAGE * HD // part):
-            sendbuf[d, :, i * part : (i + 1) * part] = nn(chosen, pmat[:, i * part : (i + 1) * part]).astype(BF16)
-        page_copy(d, 0).start()
-
-    each(answer, 1, n)
-    for c in range(1, chunks):
-        each(lambda d: page_copy(d, c).start(), 1, n)
-
     @pl.when(j == 0)
     def _():
-        prior_load.wait()
-
-        def fill(i, carry):
-            at = cols(i * HD, HD)
-            hin[:, at] = prior[at, :].T.astype(BF16)
-            return carry
-
-        lax.fori_loop(0, wide // HD, fill, 0)
         lax.fori_loop(0, parts, onward, 0)
         state_copy().start()
 
@@ -278,16 +285,9 @@
             rank = add_rank(d, rank)
     else:
         rank = lax.fori_loop(1, n, add_rank, rank)
-    lane = iota((1, lanes), 1)
-    turn = jnp.where(away == 0, 0, rank // CHUNK) * lanes + lane
-    turn_f = turn.astype(F32)
-    turn_col = jnp.broadcast_to(turn_f, (lanes, lanes)).T
-    ahead = jnp.where(turn_col < turn_f, 1.0, 0.0)
-    spot = jnp.sum(ahead, axis=0, keepdims=True).astype(jnp.int32)
-    sorted_f = jnp.where(iota((lanes, lanes), 0) == spot, 1.0, 0.0)
-    sorting = sorted_f.astype(BF16)
-    number = (lax.rem(lane, lists) * nb + lane // lists).astype(F32)
-    first_row = jnp.sum(sorted_f * number, axis=1, keepdims=True).astype(jnp.int32) * PAGE
+    page = iota((lanes, 1), 0)
+    first_row = (lax.rem(page, lists) * nb + page // lists) * PAGE
+    same = jnp.where(iota((lanes, lanes), 0) == iota((lanes, lanes), 1), 1.0, 0.0).astype(BF16)
     own_wants = onehot((slots == iota((spread_spots, lanes), 0)) & (away == 0))
     places = [onehot((rank == iota((cap, lanes), 0)) & (away == d)) for d in range(1, n)]
 
@@ -349,75 +349,78 @@
         lbuf[b] = jnp.sum(weights, axis=0, keepdims=True)
         accbuf[b] = nn(vt[:, 0:count], weights.astype(BF16))
 
-    pl.when(j >= 2)(chain)
-
-    phases = phases_of(lanes, cap)
-    arrived = 0
-    picks = []
-    for low, high, have in phases:
-        table = jnp.concatenate([own_wants] + [p[0:have] for p in places], axis=0)
-        picks.append(nt(sorting[low:high], table).astype(BF16))
+    table = jnp.concatenate([own_wants] + places, axis=0)
+    pick = nt(same, table).astype(BF16)
     if nb == 4:
         over = 1 + 2 * lax.rem(j + 1, 2)
         order = [2, over, nb - over, nb]
     else:
         order = list(range(1, nb + 1))
-    for pick, (low, high, have) in zip(picks, phases):
-        last = high == lanes
-        for c in range(arrived, have // CHUNK):
-            each(lambda d: page_copy(d, c).wait_recv(), 1, n)
-        arrived = have // CHUNK
-        pages = high - low
-        for i in range(2 * PAGE * HD // part):
-            at = slice(i * part, (i + 1) * part)
-            got = recv[1:n, 0:have, at].reshape((n - 1) * have, part)
-            out = nn(pick, jnp.concatenate([pmat[:, at], got], axis=0))
-            for k in range(2):
-                row = 2 * i + k
-                piece = out[:, k * HD : (k + 1) * HD]
-                if row < PAGE:
-                    kx[row * pages : (row + 1) * pages, 0:HD] = piece.astype(BF16)
-                    kx[row * pages : (row + 1) * pages, HD : 2 * HD] = bias(first_row[low:high] + row < prefix_limit, pages)
-                else:
-                    vstage[(row - PAGE) * pages : (row - PAGE + 1) * pages, :] = piece
-        count = PAGE * pages
-        for i in range(count // HD):
-            vt[:, i * HD : (i + 1) * HD] = vstage[i * HD : (i + 1) * HD, :].T.astype(BF16)
-
+
+    def gathered(at):
+        got = recv[1:n, :, at : at + part].reshape((n - 1) * cap, part)
+        return nn(pick, jnp.concatenate([pmat[:, at : at + part], got], axis=0))
+
+    count = PAGE * lanes
+    for i in range(PAGE):
+        kx[i * lanes : (i + 1) * lanes, HD : 2 * HD] = bias(first_row + i < prefix_limit, lanes)
+    each(lambda d: page_copy(d, 0).wait_recv(), 1, n)
+    for at in range(0, PAGE * HD, part):
+        out = gathered(at).astype(BF16)
+        i = at // HD
+        kx[i * lanes : (i + 1) * lanes, 0:HD] = out[:, 0:HD]
+        kx[(i + 1) * lanes : (i + 2) * lanes, 0:HD] = out[:, HD : 2 * HD]
+    for b in range(nb):
+        scores = nt(kx[0:count, :], queries(b))
+        old = mbuf[b]
+        top = jnp.maximum(jnp.max(scores, axis=0, keepdims=True) * rate2, old)
+        weights = jnp.exp2(scores * rate2 - top)
+        factor = jnp.exp2(old - top)
+        total = jnp.sum(weights, axis=0, keepdims=True) + lbuf[b] * factor
+        alive = b * tok + lax.rem(iota((1, rows), 1), tok) < suffix_limit
+        lbuf[b] = jnp.where(alive, 1.0 / total, 0.0)
+        accbuf[b] = accbuf[b] * factor
+        wbuf[b] = weights.astype(BF16)
+
+    pl.when(j == 2)(chain)
+
+    for s in range(PIECES):
+        if s == PIECES - 1:
+            pl.when(j > 2)(chain)
+        each(lambda d: page_copy(d, 1 + s).wait_recv(), 1, n)
+        for i in range(PAGE * PD // part):
+            out = gathered(PAGE * HD + s * PAGE * PD + i * part)
+            for t in range(2):
+                turned = out[:, t * HD : (t + 1) * HD].T.astype(BF16)
+                for k in range(PIECES):
+                    row = (2 * i + t) * PIECES + k
+                    vpart[:, row * lanes : (row + 1) * lanes] = turned[k * PD : (k + 1) * PD]
         for turn, e in enumerate(order):
             b = bpeer(e)
-            scores = nt(kx[0:count, :], queries(b))
-            old = mbuf[b]
-            top = jnp.maximum(jnp.max(scores, axis=0, keepdims=True) * rate2, old)
-            weights = jnp.exp2(scores * rate2 - top)
-            factor = jnp.exp2(old - top)
-            total = jnp.sum(weights, axis=0, keepdims=True) + lbuf[b] * factor
-            mixed = nn(vt[:, 0:count], weights.astype(BF16)) + accbuf[b] * factor
-            if not last:
-                mbuf[b] = top
-                lbuf[b] = total
-                accbuf[b] = mixed
+            final = (nn(vpart[...], wbuf[b]) + accbuf[b, s * PD : (s + 1) * PD]) * lbuf[b]
+            heads = jnp.concatenate([final[:, h * tok : (h + 1) * tok] for h in range(GROUP)], axis=0)
+            result = heads.T.astype(BF16)
+            if turn < nb - 1:
+                obuf[s, b] = result
+                out_copy(e, s).start()
             else:
-                alive = b * tok + lax.rem(iota((1, rows), 1), tok) < suffix_limit
-                final = mixed * jnp.where(alive, 1.0 / total, 0.0)
-                heads = [final[:, h * tok : (h + 1) * tok].T.astype(BF16) for h in range(GROUP)]
-                result = jnp.concatenate(heads, axis=1)
-                if turn < nb - 1:
-                    obuf[b] = result
-                    out_copy(e).start()
-                else:
-                    attn_o[:, cols(j * width, width)] = result
+                ostage[s, j] = result
 
     each_code(lambda k: code_copy(k).wait_send())
     each(lambda e: (q_copy(e).wait_send(), k_copy(e).wait_send(), v_copy(e).wait_send()), 1, nb)
-    for c in range(chunks):
+    for c in range(1 + PIECES):
         each(lambda d: page_copy(d, c).wait_send(), 1, n)
 
     @pl.when(j < nb - 1)
     def _():
         state_copy().wait_send()
 
-    each(lambda e: out_copy(e).wait(), 1, nb)
+    for s in range(PIECES):
+        each(lambda e: out_copy(e, s).wait(), 1, nb)
+    for b in range(nb):
+        for h in range(GROUP):
+            pieces = [ostage[s, b, :, h * PD : (h + 1) * PD] for s in range(PIECES)]
+            attn_o[:, b * width + h * HD : b * width + (h + 1) * HD] = jnp.concatenate(pieces, axis=1)
 
 
 def local(
@@ -438,8 +441,7 @@
     dma = pltpu.SemaphoreType.DMA
     wide = SH * HP
     rows = GROUP * tok
-    most = max([nb * tok] + [PAGE * (high - low) for low, high, _ in phases_of(lanes, cap)])
-    chunks = cap // CHUNK
+    most = max(nb * tok, PAGE * lanes)
     results = (
         jax.ShapeDtypeStruct((tok, QH * HD), BF16),
         jax.ShapeDtypeStruct((tok, wide), BF16),
@@ -462,12 +464,14 @@
             pltpu.VMEM((nb, tok, HD), BF16),
             pltpu.VMEM((nb, tok, HD), BF16),
             pltpu.VMEM((most, 2 * HD), BF16),
-            pltpu.VMEM((most, HD), F32),
-            pltpu.VMEM((HD, most), BF16),
+            pltpu.VMEM((HD, nb * tok), BF16),
+            pltpu.VMEM((PD, PAGE * lanes), BF16),
             pltpu.VMEM((nb, 1, rows), F32),
             pltpu.VMEM((nb, 1, rows), F32),
             pltpu.VMEM((nb, HD, rows), F32),
-            pltpu.VMEM((nb, tok, GROUP * HD), BF16),
+            pltpu.VMEM((nb, PAGE * lanes, rows), BF16),
+            pltpu.VMEM((PIECES, nb, tok, GROUP * PD), BF16),
+            pltpu.VMEM((PIECES, nb, tok, GROUP * PD), BF16),
             pltpu.VMEM((tok, wide), BF16),
             pltpu.VMEM((wide, NS), F32),
             pltpu.VMEM((tok, wide), F32),
@@ -476,9 +480,9 @@
             pltpu.VMEM((NS, wide), F32),
             pltpu.VMEM((NS, wide), BF16),
             pltpu.VMEM((NS, wide), BF16),
-            dma((7,)), dma((n * nb,)), dma((n * nb,)), dma((n, chunks)), dma((n, chunks)),
+            dma((7,)), dma((n * nb,)), dma((n * nb,)), dma((n, 1 + PIECES)), dma((n, 1 + PIECES)),
             dma((nb,)), dma((nb,)), dma((nb,)), dma((nb,)), dma((nb,)), dma((nb,)),
-            dma((nb,)), dma((nb,)), dma, dma,
+            dma((nb, PIECES)), dma((nb, PIECES)), dma, dma,
         ],
         compiler_params=pltpu.CompilerParams(
             collective_id=0, has_side_effects=True, vmem_limit_bytes=56 * 1024 * 1024

time: 47.2 us -> 45.2 us (0.958); the launches traced: 46.5 us -> 45 us
  Pallas kernels: 43 us -> 41.5 us
    pallas_call x1, Pallas kernels: 43 us -> 41.5 us  [local(): pl.pallas_call(functools.partial(kernel, n, nb, cap, lists, spots), out_s...]
where the time goes in v4:
time: 45.2 us; the launch traced here: 45 us
  Pallas kernels  41.5 us (92%)
  between operations  1.93 us (4%)
  local copies, waits for them, and re-layouts  1.59 us (4%)
    pallas_call x1, Pallas kernels, local(): pl.pallas_call(functools.partial(kernel, n, nb, cap, lists, spots), out_s...  41.5 us
    unnamed x2, local copies, waits for them, and re-layouts  1.59 us

profile of v4, /device:TPU:9, one launch (start us, length us, event | category | flops | bytes accessed | tf_op | source)
XLA Modules:
  0.0 45.0 jit_solution(8861244012593570843)
XLA Ops:
  1.9 41.5 %shard_map.149 = (bf16[128,2048]{1,0:T(8,128)(2,1)S(1)}, bf16[128,2048]{1,0:T(8,128)(2,1)S(1)}) custom-call(s32[1]{0:T(128)S(6)} %copy.20.plen, s32[1]{0:T(128)S(6)} %copy.21.slen, s32[1,32]{1,0:T(1,128)} %bitcast.26, s32[1,32]{1,0:T(1,128)} %bitcast.27, bf16[128,2048]{1,0:T(8,128)(2,1)} %bitcast.20, bf16[128,1024]{1,0:T(8,128)(2,1)} %bitcast.22, ...), custom_call_target="tpu_custom_call" | custom-call | tf_op jit(solution)/shard_map/pallas_call | solution.py:449
  43.4 0.8 %copy.18 = bf16[1,128,2048]{2,1,0:T(8,128)(2,1)} copy(bf16[1,128,2048]{2,1,0:T(8,128)(2,1)S(1)} %bitcast.17) | data formatting | bytes 1048576
  44.2 0.8 %copy.19 = bf16[1,128,2048]{2,1,0:T(8,128)(2,1)} copy(bf16[1,128,2048]{2,1,0:T(8,128)(2,1)S(1)} %bitcast.16) | data formatting | bytes 1048576

commit v5 on v4

--- a/solution.py
+++ b/solution.py
@@ -55,11 +55,11 @@
 
 def kernel(
     n, nb, cap, lists, spots,
-    plen, slen, owner, slot, q, kv, pool, x_hbm, b_rows, c_rows, dt_t, rate, skip, prior_hbm,
+    plen_hbm, slen_hbm, owner_hbm, slot_hbm, q, kv, pool, x_hbm, b_hbm, c_hbm, dt_hbm, rate_hbm, skip_hbm, prior_hbm,
     attn_o, ssm_o,
-    code, codes, praw, pf_k, pf_v, pmat, sendbuf, recv, qbuf, kbuf, vbuf, kx, vt, vpart, mbuf, lbuf, accbuf, wbuf, obuf, ostage,
+    plen, slen, owner, slot, b_rows, c_rows, dt_t, rate, skip, code, codes, praw, pf_k, pf_v, pmat, sendbuf, recv, qbuf, kbuf, vbuf, kx, vt, vpart, mbuf, lbuf, accbuf, wbuf, obuf, ostage,
     x, prior, afull, skipf, xp, sbuf, hin, hout,
-    loc, cs, cr, ps, pr, qs, qr, ks, kr, vs, vr, os, orr, hs, hr,
+    loc, small, cs, cr, ps, pr, qs, qr, ks, kr, vs, vr, os, orr, hs, hr,
 ):
     me = lax.axis_index("cache")
     j = lax.axis_index("blk")
@@ -69,11 +69,13 @@
     half = KVH * HD
     lanes = code.shape[1]
     rows = GROUP * tok
-    prefix_limit = plen[0]
-    suffix_limit = slen[0]
     part = 2 * HD
     parts = wide // part
 
+    def unrolled(count, body):
+        for i in range(count):
+            body(i, 0)
+
     def zpeer(d):
         return lax.rem(me + d, n)
 
@@ -81,7 +83,7 @@
         return lax.rem(j + e, nb)
 
     def cols(at, size):
-        return pl.ds(pl.multiple_of(at, 128), size)
+        return pl.ds(at if isinstance(at, int) else pl.multiple_of(at, 128), size)
 
     loads = [
         pltpu.make_async_copy(pool.at[:, cols(j * HD, HD)], praw.at[0], loc.at[0]),
@@ -94,6 +96,13 @@
     prior_load = pltpu.make_async_copy(prior_hbm, prior, loc.at[6])
     barrier = pltpu.get_barrier_semaphore()
 
+    pairs = [
+        (owner_hbm, owner), (slot_hbm, slot), (plen_hbm, plen), (slen_hbm, slen), (dt_hbm, dt_t),
+        (rate_hbm, rate), (skip_hbm, skip), (b_hbm, b_rows), (c_hbm, c_rows),
+    ]
+    fetches = [pltpu.make_async_copy(src, dst, small.at[i]) for i, (src, dst) in enumerate(pairs)]
+    fetches[0].start()
+    fetches[1].start()
     def greet(k, carry):
         peer = {"cache": zpeer(k // nb), "blk": bpeer(k % nb)}
         pl.semaphore_signal(barrier, inc=1, device_id=peer, device_id_type=pl.DeviceIdType.MESH)
@@ -105,6 +114,8 @@
     else:
         lax.fori_loop(1, n * nb, greet, 0)
     mine = iota((1, lanes), 1) // lists == j
+    fetches[0].wait()
+    fetches[1].wait()
     named_slots = slot[...] * n + owner[...]
     code[...] = jnp.where(mine, jnp.concatenate([named_slots] * nb, axis=1), 0)
     codes[me, j] = code[...]
@@ -154,7 +165,7 @@
         each(what, 1, n * nb)
 
     each_code(lambda k: code_copy(k).start())
-    for load in loads:
+    for load in loads + fetches[2:]:
         load.start()
 
     @pl.when(j == 0)
@@ -187,7 +198,7 @@
             hin[:, at] = prior[at, :].T.astype(BF16)
             return carry
 
-        lax.fori_loop(0, wide // HD, fill, 0)
+        unrolled(wide // HD, fill)
 
     before = jnp.where(iota((lanes, lanes), 0) < iota((lanes, lanes), 1), 1.0, 0.0).astype(BF16)
 
@@ -233,6 +244,10 @@
         each(answer_all, 1, n)
     each(lambda e: (k_copy(e).start(), v_copy(e).start(), q_copy(e).start()), 1, nb)
 
+    for fetch in fetches[2:]:
+        fetch.wait()
+    prefix_limit = plen[...]
+    suffix_limit = slen[...]
     dt = dt_t[...].T
     fall = jnp.concatenate(thirds(dt * (-rate[...])), axis=0).astype(BF16)
     tri = jnp.where(iota((tok, 3 * tok), 0) >= lax.rem(iota((tok, 3 * tok), 1), tok), 1.0, 0.0).astype(BF16)
@@ -259,7 +274,7 @@
         sbuf[:, at] = nn(b_t, scaled)
         return carry
 
-    lax.fori_loop(0, parts, own_block, 0)
+    unrolled(parts, own_block)
 
     def onward(i, carry):
         at = cols(i * part, part)
@@ -268,7 +283,7 @@
 
     @pl.when(j == 0)
     def _():
-        lax.fori_loop(0, parts, onward, 0)
+        unrolled(parts, onward)
         state_copy().start()
 
     owners, slots = comb(me)
@@ -301,19 +316,16 @@
             ssm_o[:, at] = jnp.where(alive, total, 0.0).astype(BF16)
             return carry
 
-        lax.fori_loop(0, parts, body, 0)
+        unrolled(parts, body)
 
     def chain():
         state_copy().wait_recv()
 
         @pl.when(j < nb - 1)
         def _():
-            lax.fori_loop(0, parts, onward, 0)
+            unrolled(parts, onward)
             state_copy().start()
 
-        read_block()
-
-    pl.when(j == 0)(read_block)
     pl.when(j == 1)(chain)
 
     rate2 = math.log2(math.e) / math.sqrt(HD)
@@ -387,6 +399,7 @@
     for s in range(PIECES):
         if s == PIECES - 1:
             pl.when(j > 2)(chain)
+            read_block()
         each(lambda d: page_copy(d, 1 + s).wait_recv(), 1, n)
         for i in range(PAGE * PD // part):
             out = gathered(PAGE * HD + s * PAGE * PD + i * part)
@@ -436,7 +449,6 @@
     spots = page_pool.shape[1]
     spread_spots = max(spots, 128)
     vmem = pl.BlockSpec(memory_space=pltpu.VMEM)
-    smem = pl.BlockSpec(memory_space=pltpu.SMEM)
     hbm = pl.BlockSpec(memory_space=pltpu.HBM)
     dma = pltpu.SemaphoreType.DMA
     wide = SH * HP
@@ -449,9 +461,18 @@
     attn, ssm = pl.pallas_call(
         functools.partial(kernel, n, nb, cap, lists, spots),
         out_shape=tuple(pltpu.VMEM(r.shape, r.dtype) for r in results),
-        in_specs=[smem, smem, vmem, vmem, hbm, hbm, hbm, hbm, vmem, vmem, vmem, vmem, vmem, hbm],
+        in_specs=[hbm] * 14,
         out_specs=(vmem, vmem),
         scratch_shapes=[
+            pltpu.VMEM((1, 1), jnp.int32),
+            pltpu.VMEM((1, 1), jnp.int32),
+            pltpu.VMEM((1, lists), jnp.int32),
+            pltpu.VMEM((1, lists), jnp.int32),
+            pltpu.VMEM((tok, NS), BF16),
+            pltpu.VMEM((tok, NS), BF16),
+            pltpu.VMEM((SH, tok), F32),
+            pltpu.VMEM((1, SH), F32),
+            pltpu.VMEM((1, SH), F32),
             pltpu.VMEM((1, lanes), jnp.int32),
             pltpu.VMEM((n, nb, 1, lanes), jnp.int32),
             pltpu.VMEM((2, spots * PAGE, HD), BF16),
@@ -480,7 +501,7 @@
             pltpu.VMEM((NS, wide), F32),
             pltpu.VMEM((NS, wide), BF16),
             pltpu.VMEM((NS, wide), BF16),
-            dma((7,)), dma((n * nb,)), dma((n * nb,)), dma((n, 1 + PIECES)), dma((n, 1 + PIECES)),
+            dma((7,)), dma((9,)), dma((n * nb,)), dma((n * nb,)), dma((n, 1 + PIECES)), dma((n, 1 + PIECES)),
             dma((nb,)), dma((nb,)), dma((nb,)), dma((nb,)), dma((nb,)), dma((nb,)),
             dma((nb, PIECES)), dma((nb, PIECES)), dma, dma,
         ],
@@ -488,7 +509,7 @@
             collective_id=0, has_side_effects=True, vmem_limit_bytes=56 * 1024 * 1024
         ),
     )(
-        prefix_len, suffix_len, page_owner[0, 0, :, 0][None], page_slot[0], queries[0], kv_new[0],
+        prefix_len[None], suffix_len[None], page_owner[0, 0, :, 0][None], page_slot[0], queries[0], kv_new[0],
         page_pool.reshape(spots * PAGE, 2 * KVH * HD), ssm_in[0], b_in[0], c_in[0], step_size[0].T,
         decay_rate[None, :], skip_gain[None, :], prior_state.reshape(wide, NS),
     )

time: 45.2 us -> 43.2 us (0.956)
  Pallas kernels: 41.5 us -> 39.5 us
    pallas_call x1, Pallas kernels: 41.5 us -> 39.5 us  [local(): pl.pallas_call(functools.partial(kernel, n, nb, cap, lists, spots), out_s...]
where the time goes in v5:
time: 43.2 us; the launch traced here: 43.1 us
  Pallas kernels  39.5 us (91%)
  between operations  1.93 us (4%)
  local copies, waits for them, and re-layouts  1.59 us (4%)
    pallas_call x1, Pallas kernels, local(): pl.pallas_call(functools.partial(kernel, n, nb, cap, lists, spots), out_s...  39.5 us
    unnamed x2, local copies, waits for them, and re-layouts  1.59 us

profile of v5, /device:TPU:9, one launch (start us, length us, event | category | flops | bytes accessed | tf_op | source)
XLA Modules:
  0.0 43.1 jit_solution(15470902250458750730)
XLA Ops:
  1.9 39.5 %shard_map.149 = (bf16[128,2048]{1,0:T(8,128)(2,1)S(1)}, bf16[128,2048]{1,0:T(8,128)(2,1)S(1)}) custom-call(s32[1,1]{1,0:T(1,128)} %bitcast.18.plen_hbm, s32[1,1]{1,0:T(1,128)} %bitcast.19.slen_hbm, s32[1,32]{1,0:T(1,128)} %bitcast.30, s32[1,32]{1,0:T(1,128)} %bitcast.31, bf16[128,2048]{1,0:T(8,128)(2,1)} %bitcast.24, bf16[128,1024]{1,0:T(8,128)(2,1)} %bitcast.26, ...), custom_call_target="tpu_custom_call" | custom-call | tf_op jit(solution)/shard_map/pallas_call | solution.py:461
  41.5 0.8 %copy.18 = bf16[1,128,2048]{2,1,0:T(8,128)(2,1)} copy(bf16[1,128,2048]{2,1,0:T(8,128)(2,1)S(1)} %bitcast.21) | data formatting | bytes 1048576
  42.3 0.8 %copy.19 = bf16[1,128,2048]{2,1,0:T(8,128)(2,1)} copy(bf16[1,128,2048]{2,1,0:T(8,128)(2,1)S(1)} %bitcast.20) | data formatting | bytes 1048576

commit v6 on v5

--- a/solution.py
+++ b/solution.py
@@ -56,7 +56,7 @@
 def kernel(
     n, nb, cap, lists, spots,
     plen_hbm, slen_hbm, owner_hbm, slot_hbm, q, kv, pool, x_hbm, b_hbm, c_hbm, dt_hbm, rate_hbm, skip_hbm, prior_hbm,
-    attn_o, ssm_o,
+    both_o,
     plen, slen, owner, slot, b_rows, c_rows, dt_t, rate, skip, code, codes, praw, pf_k, pf_v, pmat, sendbuf, recv, qbuf, kbuf, vbuf, kx, vt, vpart, mbuf, lbuf, accbuf, wbuf, obuf, ostage,
     x, prior, afull, skipf, xp, sbuf, hin, hout,
     loc, small, cs, cr, ps, pr, qs, qr, ks, kr, vs, vr, os, orr, hs, hr,
@@ -178,17 +178,9 @@
     pf_v[...] = praw[1].astype(F32)
     if spots < pmat.shape[0]:
         pmat[...] = jnp.zeros_like(pmat)
-    values = []
     for i in range(PAGE):
         at = pl.ds(i, spots, stride=PAGE)
         pmat[0:spots, i * HD : (i + 1) * HD] = pf_k[at, :].astype(BF16)
-        values.append(pf_v[at, :])
-    for s in range(PIECES):
-        for t in range(PAGE // PIECES):
-            tile = [values[t * PIECES + k][:, s * PD : (s + 1) * PD] for k in range(PIECES)]
-            at = PAGE * HD + s * PAGE * PD + t * HD
-            pmat[0:spots, at : at + HD] = jnp.concatenate(tile, axis=1).astype(BF16)
-
     @pl.when(j == 0)
     def _():
         prior_load.wait()
@@ -215,6 +207,14 @@
 
     each_code(lambda k: code_copy(k).wait_recv())
     spread_spots = pmat.shape[0]
+
+    def lay_values():
+        values = [pf_v[pl.ds(i, spots, stride=PAGE), :] for i in range(PAGE)]
+        for s in range(PIECES):
+            for t in range(PAGE // PIECES):
+                tile = [values[t * PIECES + k][:, s * PD : (s + 1) * PD] for k in range(PIECES)]
+                at = PAGE * HD + s * PAGE * PD + t * HD
+                pmat[0:spots, at : at + HD] = jnp.concatenate(tile, axis=1).astype(BF16)
 
     def chosen_for(d):
         owners, slots = comb(zpeer(d))
@@ -231,11 +231,17 @@
         page_copy(d, c).start()
 
     if n <= 8:
-        wanted = [chosen_for(d) for d in range(1, n)]
+        far = 1 + 2 * lax.rem(me + 1, 2)
+        turns = [2, far, n - far] if n == 4 else list(range(1, n))
+        wanted = [chosen_for(d) for d in turns]
         for c in range(1 + PIECES):
-            for d in range(1, n):
-                answer(d, wanted[d - 1], c)
+            if c == 1:
+                lay_values()
+            for d, chosen in zip(turns, wanted):
+                answer(d, chosen, c)
     else:
+        lay_values()
+
         def answer_all(d):
             chosen = chosen_for(d)
             for c in range(1 + PIECES):
@@ -313,7 +319,7 @@
             at = cols(i * part, part)
             both = jnp.concatenate([xp[:, at], hin[:, at]], axis=0)
             total = afull[:, at] * nn(readout, both) + skipf[0:1, at] * x[:, at].astype(F32)
-            ssm_o[:, at] = jnp.where(alive, total, 0.0).astype(BF16)
+            both_o[1, :, at] = jnp.where(alive, total, 0.0).astype(BF16)
             return carry
 
         unrolled(parts, body)
@@ -433,7 +439,7 @@
     for b in range(nb):
         for h in range(GROUP):
             pieces = [ostage[s, b, :, h * PD : (h + 1) * PD] for s in range(PIECES)]
-            attn_o[:, b * width + h * HD : b * width + (h + 1) * HD] = jnp.concatenate(pieces, axis=1)
+            both_o[0, :, b * width + h * HD : b * width + (h + 1) * HD] = jnp.concatenate(pieces, axis=1)
 
 
 def local(
@@ -454,15 +460,11 @@
     wide = SH * HP
     rows = GROUP * tok
     most = max(nb * tok, PAGE * lanes)
-    results = (
-        jax.ShapeDtypeStruct((tok, QH * HD), BF16),
-        jax.ShapeDtypeStruct((tok, wide), BF16),
-    )
-    attn, ssm = pl.pallas_call(
+    both = pl.pallas_call(
         functools.partial(kernel, n, nb, cap, lists, spots),
-        out_shape=tuple(pltpu.VMEM(r.shape, r.dtype) for r in results),
+        out_shape=pltpu.VMEM((2, tok, wide), BF16),
         in_specs=[hbm] * 14,
-        out_specs=(vmem, vmem),
+        out_specs=vmem,
         scratch_shapes=[
             pltpu.VMEM((1, 1), jnp.int32),
             pltpu.VMEM((1, 1), jnp.int32),
@@ -513,7 +515,7 @@
         page_pool.reshape(spots * PAGE, 2 * KVH * HD), ssm_in[0], b_in[0], c_in[0], step_size[0].T,
         decay_rate[None, :], skip_gain[None, :], prior_state.reshape(wide, NS),
     )
-    return attn[None], ssm[None]
+    return both[0:1], both[1:2]
 
 
 def solution(mesh):

time: 43.2 us -> 42.6 us (0.986)
  local copies, waits for them, and re-layouts: 1.59 us -> 1.08 us
    unnamed x2 -> x0, local copies, waits for them, and re-layouts: 1.59 us -> none
    slice x0 -> x1, local copies, waits for them, and re-layouts: none -> 1.08 us  [local(): return (both[0:1], both[1:2])]
where the time goes in v6:
time: 42.6 us; the launch traced here: 42.4 us
  Pallas kernels  39.4 us (92%)
  between operations  1.93 us (5%)
  local copies, waits for them, and re-layouts  1.08 us (3%)
    pallas_call x1, Pallas kernels, local(): pl.pallas_call(functools.partial(kernel, n, nb, cap, lists, spots), out_s...  39.4 us
    slice x1, local copies, waits for them, and re-layouts, local(): return (both[0:1], both[1:2])  1.08 us

profile of v6, /device:TPU:9, one launch (start us, length us, event | category | flops | bytes accessed | tf_op | source)
XLA Modules:
  0.0 42.4 jit_solution(12330282437865884045)
XLA Ops:
  1.9 39.4 %shard_map.149 = bf16[2,128,2048]{2,1,0:T(8,128)(2,1)S(1)} custom-call(s32[1,1]{1,0:T(1,128)} %bitcast.16.plen_hbm, s32[1,1]{1,0:T(1,128)} %bitcast.17.slen_hbm, s32[1,32]{1,0:T(1,128)} %bitcast.26, s32[1,32]{1,0:T(1,128)} %bitcast.27, bf16[128,2048]{1,0:T(8,128)(2,1)} %bitcast.20, bf16[128,1024]{1,0:T(8,128)(2,1)} %bitcast.22, bf16[1024,1024]{1,0:T(8,128)(2,1)} %bitcast.18, ...), custom_call_target="tpu_custom_call" | custom-call | tf_op jit(solution)/shard_map/pallas_call | solution.py:463
  41.3 1.1 %fusion = (bf16[1,128,2048]{2,1,0:T(8,128)(2,1)}, bf16[1,128,2048]{2,1,0:T(8,128)(2,1)}) fusion(bf16[2,128,2048]{2,1,0:T(8,128)(2,1)S(1)} %shard_map.149), kind=kLoop, calls=%fused_computation | loop fusion | bytes 2097152 | tf_op jit(solution)/shard_map/slice | solution.py:518

commit v7 on v6

--- a/solution.py
+++ b/solution.py
@@ -109,7 +109,7 @@
         return carry
 
     if n * nb <= 16:
-        for k in range(1, n * nb):
+        for k in list(range(nb, n * nb)) + list(range(1, nb)):
             greet(k, 0)
     else:
         lax.fori_loop(1, n * nb, greet, 0)
@@ -164,7 +164,8 @@
     def each_code(what):
         each(what, 1, n * nb)
 
-    each_code(lambda k: code_copy(k).start())
+    each(lambda k: code_copy(k).start(), nb, n * nb)
+    each(lambda k: code_copy(k).start(), 1, nb)
     for load in loads + fetches[2:]:
         load.start()
 
@@ -205,7 +206,7 @@
     def onehot(flag):
         return jnp.where(flag, 1.0, 0.0).astype(BF16)
 
-    each_code(lambda k: code_copy(k).wait_recv())
+    each(lambda k: code_copy(k).wait_recv(), nb, n * nb)
     spread_spots = pmat.shape[0]
 
     def lay_values():
@@ -291,6 +292,8 @@
     def _():
         unrolled(parts, onward)
         state_copy().start()
+
+    each(lambda k: code_copy(k).wait_recv(), 1, nb)
 
     owners, slots = comb(me)
     back = me - owners

time: 42.6 us -> 42.6 us (level)
  no operation moved by 1% of the time
where the time goes in v7:
time: 42.6 us; the launch traced here: 42.4 us
  Pallas kernels  39.4 us (92%)
  between operations  1.93 us (5%)
  local copies, waits for them, and re-layouts  1.08 us (3%)
    pallas_call x1, Pallas kernels, local(): pl.pallas_call(functools.partial(kernel, n, nb, cap, lists, spots), out_s...  39.4 us
    slice x1, local copies, waits for them, and re-layouts, local(): return (both[0:1], both[1:2])  1.08 us

profile of v7, /device:TPU:9, one launch (start us, length us, event | category | flops | bytes accessed | tf_op | source)
XLA Modules:
  0.0 42.4 jit_solution(17052163295913208747)
XLA Ops:
  1.9 39.4 %shard_map.149 = bf16[2,128,2048]{2,1,0:T(8,128)(2,1)S(1)} custom-call(s32[1,1]{1,0:T(1,128)} %bitcast.16.plen_hbm, s32[1,1]{1,0:T(1,128)} %bitcast.17.slen_hbm, s32[1,32]{1,0:T(1,128)} %bitcast.26, s32[1,32]{1,0:T(1,128)} %bitcast.27, bf16[128,2048]{1,0:T(8,128)(2,1)} %bitcast.20, bf16[128,1024]{1,0:T(8,128)(2,1)} %bitcast.22, bf16[1024,1024]{1,0:T(8,128)(2,1)} %bitcast.18, ...), custom_call_target="tpu_custom_call" | custom-call | tf_op jit(solution)/shard_map/pallas_call | solution.py:466
  41.3 1.1 %fusion = (bf16[1,128,2048]{2,1,0:T(8,128)(2,1)}, bf16[1,128,2048]{2,1,0:T(8,128)(2,1)}) fusion(bf16[2,128,2048]{2,1,0:T(8,128)(2,1)S(1)} %shard_map.149), kind=kLoop, calls=%fused_computation | loop fusion | bytes 2097152 | tf_op jit(solution)/shard_map/slice | solution.py:521
